TPU v7x, 32 devices: a whole 2x2x4 slice. The times are simulated.
32 devices in a mesh: ctx: 8 (over y, x, core), fsdp: 4 (over z).
Axes of the slice: x: 2, y: 2, z: 4, core: 2. Of those that a mesh axis runs over, the one named last changes fastest.
Arguments:
- tokens: bfloat16 [4, 1024, 768], P('fsdp', 'ctx'), may hold values from -6 to 6
- cotangent: bfloat16 [4, 1024, 768], P('fsdp', 'ctx'), may hold values from -6 to 6
- att_gain: bfloat16 [768], P('fsdp'), may hold values from 0.25 to 1.75
- att_shift: bfloat16 [768], P('fsdp'), may hold values from -1.75 to 1.75
- ffn_gain: bfloat16 [768], P('fsdp'), may hold values from 0.25 to 1.75
- ffn_shift: bfloat16 [768], P('fsdp'), may hold values from -1.75 to 1.75
- qkv_weight: bfloat16 [768, 2304], P('fsdp'), may hold values from -0.3125 to 0.3125
- qkv_bias: bfloat16 [2304], P('fsdp'), may hold values from -3 to 3
- out_weight: bfloat16 [768, 768], P('fsdp'), may hold values from -0.875 to 0.875
- out_bias: bfloat16 [768], P('fsdp'), may hold values from -3 to 3
- up_weight: bfloat16 [768, 3072], P(None, 'fsdp'), may hold values from -0.21875 to 0.21875
- up_bias: bfloat16 [3072], P('fsdp'), may hold values from -3 to 3
- down_weight: bfloat16 [3072, 768], P('fsdp'), may hold values from -0.109375 to 0.109375
- down_bias: bfloat16 [768], P('fsdp'), may hold values from -3 to 3
Outputs:
- layer_out: bfloat16 [4, 1024, 768], P('fsdp', 'ctx')
- input_grad: float32 [4, 1024, 768], P('fsdp', 'ctx')
- att_dgain: float32 [768], P('fsdp')
- att_dshift: float32 [768], P('fsdp')
- ffn_dgain: float32 [768], P('fsdp')
- ffn_dshift: float32 [768], P('fsdp')
- qkv_dweight: float32 [768, 2304], P('fsdp')
- qkv_dbias: float32 [2304], P('fsdp')
- out_dweight: float32 [768, 768], P('fsdp')
- out_dbias: float32 [768], P('fsdp')
- up_dweight: float32 [768, 3072], P(None, 'fsdp')
- up_dbias: float32 [3072], P('fsdp')
- down_dweight: float32 [3072, 768], P('fsdp')
- down_dbias: float32 [768], P('fsdp')
All inputs are finite; a program needn't handle non-finite values.
Results may differ from a plain program's by a relative error of at most 0.012.
The roundings to bfloat16 on the way count: a program that leaves them out, or rounds other values in their place, can miss the bound.
Values may be sent and summed in bfloat16 or wider, within the bound.
No kernel may reach another device: no remote copies, remote signals or barrier semaphores. Data moves between devices by JAX's collectives and lax.ppermute only.
A program may use at most 192 MiB of HBM per device.

v0:
```python
import math

import jax
import jax.numpy as jnp
from jax import lax
from jax.experimental import pallas as pl
from jax.experimental.pallas import tpu as pltpu
from jax.sharding import PartitionSpec as P
import numpy as np

HEADS = 12
HEAD_DIM = 64
ROT_DIMS = 16


def layer_norm(values, norm_gain, norm_shift):
    center = values - jnp.mean(values, axis=-1, keepdims=True)
    spread = jnp.mean(center * center, axis=-1, keepdims=True)
    return center * lax.rsqrt(spread + 1e-05) * norm_gain + norm_shift


def exact_gelu(values):
    return jax.nn.gelu(values, approximate=False)


def stored_positions(rows, devices):
    row_order = jnp.arange(rows * devices, dtype=jnp.int32)
    device = row_order // rows
    within = row_order % rows
    half_rows = rows // 2
    return jnp.where(
        within < half_rows,
        device * half_rows + within,
        (2 * devices - 1 - device) * half_rows + within - half_rows,
    )


def rotary_angles(positions):
    half_rot = ROT_DIMS // 2
    inverse = jnp.power(10000.0, -2.0 * jnp.arange(half_rot, dtype=jnp.float32) / ROT_DIMS)
    return positions.astype(jnp.float32)[:, None] * inverse[None, :]


def rotate(heads, angles):
    half_rot = ROT_DIMS // 2
    cosine = jnp.cos(angles)[:, None, :]
    sine_part = jnp.sin(angles)[:, None, :]
    lower_half = heads[..., :half_rot]
    upper_half = heads[..., half_rot:ROT_DIMS]
    return jnp.concatenate(
        [
            lower_half * cosine - upper_half * sine_part,
            upper_half * cosine + lower_half * sine_part,
            heads[..., ROT_DIMS:],
        ],
        axis=-1,
    )


def to_order(stack, ctx_count, half_rows):
    tail = stack.shape[1:]
    shaped = stack.reshape((ctx_count, 2, half_rows) + tail)
    return jnp.concatenate(
        [shaped[:, 0].reshape((-1,) + tail), shaped[::-1, 1].reshape((-1,) + tail)], axis=0
    )


def from_order(stack, ctx_count, half_rows):
    tail = stack.shape[1:]
    middle = stack.shape[0] // 2
    first = stack[:middle].reshape((ctx_count, half_rows) + tail)
    second = stack[middle:].reshape((ctx_count, half_rows) + tail)[::-1]
    return jnp.stack([first, second], axis=1).reshape(stack.shape)


def scores_block(query_heads, key_heads, query_pos, key_pos):
    scores = jnp.einsum(
        "qhd,khd->hqk", query_heads, key_heads, preferred_element_type=jnp.float32
    ) / math.sqrt(HEAD_DIM)
    return jnp.where(key_pos[None, None, :] <= query_pos[None, :, None], scores, -1000000000.0)


def grad_block(
    query_heads, grad_heads, log_total, inner, query_pos, key_heads, value_heads, key_pos
):
    scores = scores_block(query_heads, key_heads, query_pos, key_pos)
    probability = jnp.exp(scores - log_total[:, :, None])
    prob_grad = jnp.einsum(
        "qhd,khd->hqk", grad_heads, value_heads, preferred_element_type=jnp.float32
    )
    score_grad = (probability * (prob_grad - inner[:, :, None])).astype(jnp.bfloat16)
    return (probability.astype(jnp.bfloat16), score_grad)


def shards(
    tokens,
    cotangent,
    att_gain,
    att_shift,
    ffn_gain,
    ffn_shift,
    qkv_weight,
    qkv_bias,
    out_weight,
    out_bias,
    up_weight,
    up_bias,
    down_weight,
    down_bias,
):
    model_width = tokens.shape[-1]
    rows_in = tokens.reshape(-1, model_width)
    grad_rows = cotangent.reshape(-1, model_width)
    own_rows = rows_in.shape[0]
    half_rows = own_rows // 2
    ctx_count = lax.axis_size("ctx")
    ctx_place = lax.axis_index("ctx")
    total_rows = own_rows * ctx_count
    all_pos = stored_positions(own_rows, ctx_count)
    own_pos = lax.dynamic_slice_in_dim(all_pos, ctx_place * own_rows, own_rows, 0)
    (
        gain_attend,
        shift_attend,
        gain_feed,
        shift_feed,
        mat_qkv,
        bias_qkv,
        mat_out,
        bias_out,
        bias_down,
    ) = (
        lax.all_gather(att_gain, "fsdp", axis=0, tiled=True),
        lax.all_gather(att_shift, "fsdp", axis=0, tiled=True),
        lax.all_gather(ffn_gain, "fsdp", axis=0, tiled=True),
        lax.all_gather(ffn_shift, "fsdp", axis=0, tiled=True),
        lax.all_gather(qkv_weight, "fsdp", axis=0, tiled=True),
        lax.all_gather(qkv_bias, "fsdp", axis=0, tiled=True),
        lax.all_gather(out_weight, "fsdp", axis=0, tiled=True),
        lax.all_gather(out_bias, "fsdp", axis=0, tiled=True),
        lax.all_gather(down_bias, "fsdp", axis=0, tiled=True),
    )
    tokens32 = rows_in.astype(jnp.float32)
    grad32 = grad_rows.astype(jnp.float32)
    first_norm, first_back = jax.vjp(
        layer_norm, tokens32, gain_attend.astype(jnp.float32), shift_attend.astype(jnp.float32)
    )
    second_norm, second_back = jax.vjp(
        layer_norm, tokens32, gain_feed.astype(jnp.float32), shift_feed.astype(jnp.float32)
    )
    first_in = first_norm.astype(jnp.bfloat16)
    second_in = second_norm.astype(jnp.bfloat16)
    joined = jnp.dot(first_in, mat_qkv, preferred_element_type=jnp.float32) + bias_qkv.astype(
        jnp.float32
    )
    angles = rotary_angles(own_pos)

    def project_heads(joined_rows):
        queries = rotate(joined_rows[:, :model_width].reshape(own_rows, HEADS, HEAD_DIM), angles)
        keys_rot = rotate(
            joined_rows[:, model_width : 2 * model_width].reshape(own_rows, HEADS, HEAD_DIM), angles
        )
        return (
            queries.reshape(own_rows, model_width),
            keys_rot.reshape(own_rows, model_width),
            joined_rows[:, 2 * model_width :],
        )

    (queries, keys_rot, values_rows), rotary_back = jax.vjp(project_heads, joined)
    query_low = queries.astype(jnp.bfloat16)
    key_low = keys_rot.astype(jnp.bfloat16)
    value_low = values_rows.astype(jnp.bfloat16)
    key_all, value_all = (
        lax.all_gather(key_low, "ctx", axis=0, tiled=True),
        lax.all_gather(value_low, "ctx", axis=0, tiled=True),
    )
    query_heads = query_low.reshape(own_rows, HEADS, HEAD_DIM)
    key_heads = to_order(key_all, ctx_count, half_rows).reshape(total_rows, HEADS, HEAD_DIM)
    value_heads = to_order(value_all, ctx_count, half_rows).reshape(total_rows, HEADS, HEAD_DIM)
    block_keys = min(1024, total_rows)

    def key_piece(block_index):
        start = block_index * block_keys
        return (
            lax.dynamic_slice_in_dim(key_heads, start, block_keys, 0),
            lax.dynamic_slice_in_dim(value_heads, start, block_keys, 0),
            start + jnp.arange(block_keys, dtype=jnp.int32),
        )

    need_low = (ctx_place + 1) * half_rows
    need_high = (2 * ctx_count - ctx_place) * half_rows
    counts = ((need_low + block_keys - 1) // block_keys, (need_high + block_keys - 1) // block_keys)
    query_parts = (query_heads[:half_rows], query_heads[half_rows:])
    pos_parts = (own_pos[:half_rows], own_pos[half_rows:])

    def half_lse(query_half, pos_half, count):

        def lse_step(block_index, carried):
            row_top, exp_total = carried
            key_block, value_skip, key_pos = key_piece(block_index)
            scores = scores_block(query_half, key_block, pos_half, key_pos)
            new_top = jnp.maximum(row_top, jnp.max(scores, axis=-1))
            exp_total = exp_total * jnp.exp(row_top - new_top) + jnp.sum(
                jnp.exp(scores - new_top[:, :, None]), axis=-1
            )
            return (new_top, exp_total)

        start_top = jnp.full((HEADS, half_rows), -1e30, jnp.float32)
        start_sum = jnp.zeros((HEADS, half_rows), jnp.float32)
        row_top, exp_total = lax.fori_loop(0, count, lse_step, (start_top, start_sum))
        return row_top + jnp.log(exp_total)

    lse_parts = [
        half_lse(query_parts[half_index], pos_parts[half_index], counts[half_index])
        for half_index in range(2)
    ]

    def half_mix(query_half, pos_half, lse_half, count):

        def mix_step(block_index, totals):
            key_block, value_block, key_pos = key_piece(block_index)
            scores = scores_block(query_half, key_block, pos_half, key_pos)
            probability = jnp.exp(scores - lse_half[:, :, None]).astype(jnp.bfloat16)
            return totals + jnp.einsum(
                "hqk,khd->qhd", probability, value_block, preferred_element_type=jnp.float32
            )

        return lax.fori_loop(
            0, count, mix_step, jnp.zeros((half_rows, HEADS, HEAD_DIM), jnp.float32)
        )

    attended = jnp.concatenate(
        [
            half_mix(
                query_parts[half_index],
                pos_parts[half_index],
                lse_parts[half_index],
                counts[half_index],
            )
            for half_index in range(2)
        ],
        axis=0,
    )
    attended_low = attended.reshape(own_rows, model_width).astype(jnp.bfloat16)
    branch_att = jnp.dot(
        attended_low, mat_out, preferred_element_type=jnp.float32
    ) + bias_out.astype(jnp.float32)
    second_all, grad_all = (
        lax.all_gather(second_in, "fsdp", axis=0, tiled=True),
        lax.all_gather(grad_rows, "fsdp", axis=0, tiled=True),
    )
    hidden = jnp.dot(second_all, up_weight, preferred_element_type=jnp.float32) + up_bias.astype(
        jnp.float32
    )
    active, gelu_back = jax.vjp(exact_gelu, hidden)
    active_low = active.astype(jnp.bfloat16)
    ffn_part = jnp.dot(active_low, down_weight, preferred_element_type=jnp.float32)
    active_grad = jnp.einsum("te,fe->tf", grad_all, down_weight, preferred_element_type=jnp.float32)
    hidden_grad = gelu_back(active_grad)[0].astype(jnp.bfloat16)
    down_dweight = jnp.einsum("tf,te->fe", active_low, grad_all, preferred_element_type=jnp.float32)
    up_dweight = jnp.einsum(
        "td,tf->df", second_all, hidden_grad, preferred_element_type=jnp.float32
    )
    up_dbias = jnp.sum(hidden_grad.astype(jnp.float32), axis=0)
    second_part = jnp.einsum(
        "tf,df->td", hidden_grad, up_weight, preferred_element_type=jnp.float32
    )
    ffn_sum, second_grad = (
        lax.psum_scatter(ffn_part, "fsdp", scatter_dimension=0, tiled=True),
        lax.psum_scatter(second_part, "fsdp", scatter_dimension=0, tiled=True),
    )
    branch_ffn = ffn_sum + bias_down.astype(jnp.float32)
    layer_out = (tokens32 + branch_att + branch_ffn).astype(jnp.bfloat16).reshape(tokens.shape)
    out_dweight = jnp.einsum(
        "td,te->de", attended_low, grad_rows, preferred_element_type=jnp.float32
    )
    row_sum = jnp.sum(grad32, axis=0)
    attended_grad = jnp.einsum(
        "te,de->td", grad_rows, mat_out, preferred_element_type=jnp.float32
    ).astype(jnp.bfloat16)
    grad_heads = attended_grad.reshape(own_rows, HEADS, HEAD_DIM)
    grad_parts = (grad_heads[:half_rows], grad_heads[half_rows:])

    def half_inner(query_half, grad_half, pos_half, lse_half, count):

        def inner_step(block_index, totals):
            key_block, value_block, key_pos = key_piece(block_index)
            scores = scores_block(query_half, key_block, pos_half, key_pos)
            probability = jnp.exp(scores - lse_half[:, :, None])
            prob_grad = jnp.einsum(
                "qhd,khd->hqk", grad_half, value_block, preferred_element_type=jnp.float32
            )
            return totals + jnp.sum(probability * prob_grad, axis=-1)

        return lax.fori_loop(0, count, inner_step, jnp.zeros((HEADS, half_rows), jnp.float32))

    inner_parts = [
        half_inner(
            query_parts[half_index],
            grad_parts[half_index],
            pos_parts[half_index],
            lse_parts[half_index],
            counts[half_index],
        )
        for half_index in range(2)
    ]
    half_zeros = jnp.zeros((half_rows, HEADS, HEAD_DIM), jnp.float32)

    def half_back(half_index, carried):
        query_half = query_parts[half_index]
        grad_half = grad_parts[half_index]

        def query_step(block_index, state):
            query_total, key_acc, value_acc = state
            key_block, value_block, key_pos = key_piece(block_index)
            prob_low, score_grad = grad_block(
                query_half,
                grad_half,
                lse_parts[half_index],
                inner_parts[half_index],
                pos_parts[half_index],
                key_block,
                value_block,
                key_pos,
            )
            key_part = jnp.einsum(
                "hqk,qhd->khd", score_grad, query_half, preferred_element_type=jnp.float32
            )
            value_part = jnp.einsum(
                "hqk,qhd->khd", prob_low, grad_half, preferred_element_type=jnp.float32
            )
            start = block_index * block_keys
            key_acc = lax.dynamic_update_slice_in_dim(
                key_acc,
                lax.dynamic_slice_in_dim(key_acc, start, block_keys, 0) + key_part,
                start,
                0,
            )
            value_acc = lax.dynamic_update_slice_in_dim(
                value_acc,
                lax.dynamic_slice_in_dim(value_acc, start, block_keys, 0) + value_part,
                start,
                0,
            )
            query_total = query_total + jnp.einsum(
                "hqk,khd->qhd", score_grad, key_block, preferred_element_type=jnp.float32
            )
            return (query_total, key_acc, value_acc)

        return lax.fori_loop(0, counts[half_index], query_step, carried)

    full_zeros = jnp.zeros((total_rows, HEADS, HEAD_DIM), jnp.float32)
    query_low_sum, key_acc, value_acc = half_back(0, (half_zeros, full_zeros, full_zeros))
    query_high_sum, key_acc, value_acc = half_back(1, (half_zeros, key_acc, value_acc))
    query_sum = jnp.concatenate([query_low_sum, query_high_sum], axis=0)
    key_stored = from_order(key_acc.reshape(total_rows, model_width), ctx_count, half_rows)
    value_stored = from_order(value_acc.reshape(total_rows, model_width), ctx_count, half_rows)
    key_sum, value_sum = (
        lax.psum_scatter(key_stored, "ctx", scatter_dimension=0, tiled=True),
        lax.psum_scatter(value_stored, "ctx", scatter_dimension=0, tiled=True),
    )
    query_grad = query_sum.reshape(own_rows, model_width) / math.sqrt(HEAD_DIM)
    key_grad = key_sum / math.sqrt(HEAD_DIM)
    joined_grad = rotary_back((query_grad, key_grad, value_sum))[0].astype(jnp.bfloat16)
    qkv_dweight = jnp.einsum("td,tf->df", first_in, joined_grad, preferred_element_type=jnp.float32)
    qkv_dbias = jnp.sum(joined_grad.astype(jnp.float32), axis=0)
    first_grad = jnp.einsum("tf,df->td", joined_grad, mat_qkv, preferred_element_type=jnp.float32)
    token_first, att_dgain, att_dshift = first_back(first_grad)
    token_second, ffn_dgain, ffn_dshift = second_back(second_grad)
    input_grad = (grad32 + token_first + token_second).reshape(tokens.shape)
    shares = (
        lax.psum_scatter(att_dgain, "fsdp", scatter_dimension=0, tiled=True),
        lax.psum_scatter(att_dshift, "fsdp", scatter_dimension=0, tiled=True),
        lax.psum_scatter(ffn_dgain, "fsdp", scatter_dimension=0, tiled=True),
        lax.psum_scatter(ffn_dshift, "fsdp", scatter_dimension=0, tiled=True),
        lax.psum_scatter(qkv_dweight, "fsdp", scatter_dimension=0, tiled=True),
        lax.psum_scatter(qkv_dbias, "fsdp", scatter_dimension=0, tiled=True),
        lax.psum_scatter(out_dweight, "fsdp", scatter_dimension=0, tiled=True),
        lax.psum_scatter(row_sum, "fsdp", scatter_dimension=0, tiled=True),
    ) + (up_dweight, up_dbias, down_dweight)
    totals = lax.psum(
        (
            shares[0],
            shares[1],
            shares[2],
            shares[3],
            shares[4],
            shares[5],
            shares[6],
            shares[7],
            shares[8],
            shares[9],
            shares[10],
        ),
        "ctx",
    )
    return (
        layer_out,
        input_grad,
        totals[0],
        totals[1],
        totals[2],
        totals[3],
        totals[4],
        totals[5],
        totals[6],
        totals[7],
        totals[8],
        totals[9],
        totals[10],
        totals[7],
    )


F32 = jnp.float32
BF16 = jnp.bfloat16
GROUPS = 4
GROUP_HEADS = HEADS // GROUPS
GROUP_COLS = GROUP_HEADS * HEAD_DIM
EXTRA = 16


def fits(mesh):
    return mesh.shape["ctx"] == 2 * GROUPS and mesh.shape["fsdp"] == GROUPS


def mm(left, right):
    return jnp.dot(left, right, preferred_element_type=F32)


def mm_nt(left, right):
    return lax.dot_general(left, right, (((1,), (1,)), ((), ())), preferred_element_type=F32)


def mm_tn(left, right):
    return lax.dot_general(left, right, (((0,), (0,)), ((), ())), preferred_element_type=F32)


def local_call(
    name, body, places, ins, outs, scratch=(), flops=0, whole=(), after=(), through=(), vmem=28
):
    waits = len(after) + len(through)
    inner, first, last = body, 1 + waits, 1 + waits + len(ins) + len(whole)

    def body(*refs):
        given = refs[first:last]
        given = given[len(whole) :][::-1] + given[: len(whole)][::-1]
        made = refs[last : last + len(outs)]
        inner(refs[0], *given, *made, *refs[last + len(outs) + len(through) :])

    moved = sum(math.prod(i.shape) * i.dtype.itemsize for i in ins)
    moved += sum(math.prod(s) * jnp.dtype(d).itemsize for s, d in outs)
    return pl.pallas_call(
        body,
        out_shape=[jax.ShapeDtypeStruct(s, d) for s, d in outs]
        + [jax.ShapeDtypeStruct(t.shape, t.dtype) for t in through],
        in_specs=[pl.BlockSpec(memory_space=pltpu.SMEM)]
        + [pl.BlockSpec(memory_space=pl.ANY)] * (waits + len(whole))
        + [pl.BlockSpec(memory_space=pltpu.VMEM)] * len(ins),
        out_specs=[pl.BlockSpec(memory_space=pltpu.VMEM)] * len(outs)
        + [pl.BlockSpec(memory_space=pl.ANY)] * len(through),
        input_output_aliases={1 + len(after) + i: len(outs) + i for i in range(len(through))},
        scratch_shapes=list(scratch),
        compiler_params=pltpu.CompilerParams(vmem_limit_bytes=vmem * 2**20),
        cost_estimate=pl.CostEstimate(flops=flops, bytes_accessed=moved, transcendentals=0),
        name=name,
    )(places, *after, *through, *whole[::-1], *ins[::-1])


def normed(values):
    center = values - jnp.mean(values, axis=-1, keepdims=True)
    spread = jnp.mean(center * center, axis=-1, keepdims=True)
    scale = lax.rsqrt(spread + 1e-05)
    return center * scale, scale


def rotary_tables(rows, devices):
    half = rows // 2
    order = np.arange(rows * devices)
    device, within = order // rows, order % rows
    position = np.where(
        within < half, device * half + within, (2 * devices - 1 - device) * half + within - half
    )
    pairs = ROT_DIMS // 2
    inverse = np.power(10000.0, -2.0 * np.arange(pairs) / ROT_DIMS).astype(np.float32)
    angle = (position.astype(np.float32)[:, None] * inverse[None, :]).astype(np.float32)
    cosine = np.ones((rows * devices, HEAD_DIM), np.float32)
    sine = np.zeros((rows * devices, HEAD_DIM), np.float32)
    cosine[:, :pairs] = cosine[:, pairs:ROT_DIMS] = np.cos(angle)
    sine[:, :pairs] = -np.sin(angle)
    sine[:, pairs:ROT_DIMS] = np.sin(angle)
    return np.tile(cosine, (1, 2)), np.tile(sine, (1, 2))


def swapped(values):
    lanes = values.shape[1]
    place = lax.broadcasted_iota(jnp.int32, values.shape, 1) % HEAD_DIM
    return jnp.where(
        place < ROT_DIMS // 2,
        pltpu.roll(values, lanes - ROT_DIMS // 2, 1),
        pltpu.roll(values, ROT_DIMS // 2, 1),
    )


def pack_body(places, *refs):
    vectors, (qkv_w, x, g, out_w) = refs[0:7], refs[7:11]
    payload, xg, xg_line, out_half, box, rows_w, sems = refs[11:]
    core, group = places[0] % 2, places[0] // 2
    part = rows_w.shape[0]
    width = xg.shape[1]
    rows = x.shape[0]
    copies = [
        pltpu.make_async_copy(
            qkv_w.at[pl.ds(pl.multiple_of(core * part, part), part), :], rows_w, sems.at[0]
        ),
        pltpu.make_async_copy(x, xg.at[pl.ds(0, rows), :], sems.at[1]),
        pltpu.make_async_copy(g, xg.at[pl.ds(rows, rows), :], sems.at[2]),
        pltpu.make_async_copy(
            out_w.at[pl.ds(pl.multiple_of(core * part, part), part), :], out_half, sems.at[3]
        ),
        pltpu.make_async_copy(x, xg_line.at[pl.ds(0, rows), :], sems.at[4]),
        pltpu.make_async_copy(g, xg_line.at[pl.ds(rows, rows), :], sems.at[5]),
    ]
    for copy in copies:
        copy.start()
    box[...] = jnp.zeros_like(box)
    shard = vectors[0].shape[0]
    for item in range(6):
        box[item // 3 : item // 3 + 1, (item % 3) * shard : (item % 3 + 1) * shard] = (
            vectors[item][...].astype(F32).reshape(1, shard)
        )
    box[2:3, :] = vectors[6][...].astype(F32).reshape(1, 3 * shard)
    payload[part:, :] = box[...].astype(BF16)
    copies[0].wait()
    for owner in range(GROUPS):

        @pl.when(group == owner)
        def _():
            for slot, base in enumerate((1, 0, 2)):
                at = base * width + owner * GROUP_COLS
                payload[0:part, slot * GROUP_COLS : (slot + 1) * GROUP_COLS] = rows_w[
                    :, at : at + GROUP_COLS
                ]

    for copy in copies[1:]:
        copy.wait()


def collect_body(places, p0, p1, p2, p3, stack, vec, bias, box):
    z, group = places[1], places[0] // 2
    part = p0.shape[0] - EXTRA
    three = p0.shape[1]
    shard = vec.shape[1] // GROUPS
    for k, piece in enumerate((p0, p1, p2, p3)):
        stack[k * part : (k + 1) * part, :] = piece[0:part, :]
        box[z ^ k] = piece[part:, :].astype(F32)
    units = []
    for owner in range(GROUPS):
        block = box[owner]
        for item in range(6):
            vec[item : item + 1, owner * shard : (owner + 1) * shard] = block[
                item // 3 : item // 3 + 1, (item % 3) * shard : (item % 3 + 1) * shard
            ]
        for unit in range(3):
            units.append(block[2:3, unit * GROUP_COLS : (unit + 1) * GROUP_COLS])
    for slot, base in enumerate((GROUPS, 0, 2 * GROUPS)):
        own = units[base]
        for g in range(1, GROUPS):
            own = jnp.where(group == g, units[base + g], own)
        bias[0:1, slot * GROUP_COLS : (slot + 1) * GROUP_COLS] = own


def qkv_body(places, *refs):
    xs, (near, far, vec, bias, cos_tab, sin_tab) = refs[0:4], refs[4:10]
    fi, w, q_out, kv_out, cos, sin = refs[10:]
    c, z = places[0], places[1]
    core = c % 2
    width = w.shape[0]
    shard = width // GROUPS
    part = shard // 2
    rows = xs[0].shape[0] // 2
    half = rows // 2
    near_rows = GROUPS * rows
    for side, stack in ((core, near), (1 - core, far)):
        for k in range(GROUPS):
            base = (z ^ k) * shard + side * part
            w[pl.ds(pl.multiple_of(base, part), part), :] = stack[k * part : (k + 1) * part, :]
    gain, shift = vec[0:1, :], vec[1:2, :]
    two = 2 * GROUP_COLS
    for side in range(2):
        for j in range(GROUPS):
            source = c ^ (2 * j)
            to = slice((side * GROUPS + j) * half, (side * GROUPS + j + 1) * half)
            at = pl.ds(pl.multiple_of(source * rows + side * half, half), half)
            norm, _ = normed(xs[j][side * half : (side + 1) * half, :].astype(F32))
            fi[to, :] = (norm * gain + shift).astype(BF16)
            cos[to, :] = cos_tab[at, :]
            sin[to, :] = sin_tab[at, :]
    step = 2 * rows
    for i in range(near_rows // step):
        at = slice(i * step, (i + 1) * step)
        chunk = fi[at, :]
        kq = mm(chunk, w[:, :two]) + bias[0:1, :two]
        c3 = jnp.concatenate([cos[at, :]] * 3, axis=1)
        s3 = jnp.concatenate([sin[at, :]] * 3, axis=1)
        kq = kq * c3 + swapped(kq) * s3
        kv_out[at, :] = kq[:, :GROUP_COLS].astype(BF16)
        q_out[at, :] = (kq[:, GROUP_COLS:] * HEAD_DIM**-0.5).astype(BF16)
        kv_out[near_rows + i * step : near_rows + (i + 1) * step, :] = (
            mm(chunk, w[:, two:]) + bias[0:1, two:]
        ).astype(BF16)


def key_order(kv, kv_far, kbuf, vbuf, low):
    near_rows = 2 * low
    for side in range(2):
        for part, source in enumerate((kv, kv_far)):
            to = slice((2 * side + part) * low, (2 * side + part + 1) * low)
            kbuf[to, :] = source[side * low : (side + 1) * low, :]
            vbuf[to, :] = source[near_rows + side * low : near_rows + (side + 1) * low, :]


def visible(c, low):
    half = low // GROUPS
    devices = 2 * GROUPS

    def token_pos(index, far):
        device = (c ^ (2 * (index // half))) ^ far
        return device * half + index % half

    q_place = token_pos(lax.broadcasted_iota(jnp.int32, (low, 1), 0), 0)
    k_index = lax.broadcasted_iota(jnp.int32, (1, 2 * low), 1)
    k_place = token_pos(k_index % low, k_index // low)

    def mirrored(place):
        return (2 * devices - 1 - place // half) * half + place % half

    return (k_place <= q_place, mirrored(k_place) <= mirrored(q_place))


def masked_scores(query, keys, side, spans, allowed):
    scores = [mm_nt(query, keys[s]) for s in spans]
    scores[-1] = jnp.where(allowed[side], scores[-1], -1000000000.0)
    return scores


def key_spans(side, low):
    return [slice(0, 2 * low), slice(2 * low, 4 * low)][: side + 1]


def attend_body(places, *refs):
    q, kv, kv_far = refs[0:3]
    xgs, (ow_near, ow_far) = refs[3:7], refs[7:9]
    sends, (dkq, dv_out, far_out) = refs[9:13], refs[13:16]
    kbuf, vbuf, att, ag, ow, g_half, pieces = refs[16:]
    c, z = places[0], places[1]
    core = c % 2
    rows = sends[0].shape[0]
    near_rows = GROUPS * rows
    half = rows // 2
    low = GROUPS * half
    part = GROUP_COLS // 2
    key_order(kv, kv_far, kbuf, vbuf, low)
    ow[pl.ds(pl.multiple_of(core * part, part), part), :] = ow_near[...]
    ow[pl.ds(pl.multiple_of((1 - core) * part, part), part), :] = ow_far[...]
    for side in range(2):
        for j in range(GROUPS):
            g_half[(side * GROUPS + j) * half : (side * GROUPS + j + 1) * half, :] = xgs[j][
                rows + side * half : rows + (side + 1) * half, :
            ]
    ag[...] = mm_nt(g_half[...], ow[...]).astype(BF16)
    allowed = visible(c, low)
    for head in range(GROUP_HEADS):
        lanes = slice(head * HEAD_DIM, (head + 1) * HEAD_DIM)
        lanes2 = slice(GROUP_COLS + head * HEAD_DIM, GROUP_COLS + (head + 1) * HEAD_DIM)
        kh, vh = kbuf[:, lanes], vbuf[:, lanes]
        dk_parts, dv_parts = [], []
        for side in range(2):
            at = slice(side * low, (side + 1) * low)
            qh, gh = q[at, lanes], ag[at, lanes]
            spans = [slice(0, 2 * low), slice(2 * low, 4 * low)][: side + 1]
            scores = [mm_nt(qh, kh[s]) for s in spans]
            scores[-1] = jnp.where(allowed[side], scores[-1], -1000000000.0)
            top = jnp.max(scores[0], axis=-1, keepdims=True)
            for s in scores[1:]:
                top = jnp.maximum(top, jnp.max(s, axis=-1, keepdims=True))
            raised = [jnp.exp(s - top) for s in scores]
            inverse = 1.0 / sum(jnp.sum(r, axis=-1, keepdims=True) for r in raised)
            probs = [r * inverse for r in raised]
            low_probs = [p.astype(BF16) for p in probs]
            mixed = sum(mm(p, vh[s]) for p, s in zip(low_probs, spans))
            att[at, lanes] = mixed.astype(BF16)
            prob_grads = [mm_nt(gh, vh[s]) for s in spans]
            inner = sum(
                jnp.sum(p * d, axis=-1, keepdims=True) for p, d in zip(probs, prob_grads)
            )
            score_grads = [(p * (d - inner)).astype(BF16) for p, d in zip(probs, prob_grads)]
            dkq[at, lanes2] = sum(mm(s, kh[a]) for s, a in zip(score_grads, spans)) * HEAD_DIM**-0.5
            dk_parts.append([mm_tn(s, qh) for s in score_grads])
            dv_parts.append([mm_tn(p, gh) for p in low_probs])
        dk = (dk_parts[0][0] + dk_parts[1][0], dk_parts[1][1])
        dv = (dv_parts[0][0] + dv_parts[1][0], dv_parts[1][1])
        for side in range(2):
            at = slice(side * low, (side + 1) * low)
            dkq[at, lanes] = dk[side][:low]
            dv_out[at, lanes] = dv[side][:low]
            far_out[at, lanes] = dk[side][low:].astype(BF16)
            far_out[at, lanes2] = dv[side][low:].astype(BF16)
    for side in range(2):
        for j in range(GROUPS):
            pieces[j, side * half : (side + 1) * half, :] = att[
                (side * GROUPS + j) * half : (side * GROUPS + j + 1) * half, :
            ]
    for m in range(GROUPS):
        sends[m][...] = pieces[(c // 2) ^ z ^ m]


def joined_body(places, *refs):
    dkq, dv, far, w, fi, cos, sin, vec = refs[0:8]
    xs, g_own = refs[8:12], refs[12]
    ca, sends, keep, send = refs[13], refs[14:17], refs[17], refs[18]
    jgkq, jgv, dwbuf, first, ext = refs[19:]
    c, z = places[0], places[1]
    core, group = c % 2, c // 2
    rows = ca.shape[0]
    half = rows // 2
    width = w.shape[0]
    shard = width // GROUPS
    part = shard // 2
    two = 2 * GROUP_COLS
    step = 2 * rows
    gain = vec[0:1, :]
    bias_kq = jnp.zeros((1, two), F32)
    bias_v = jnp.zeros((1, GROUP_COLS), F32)
    for i in range(GROUPS * rows // step):
        at = slice(i * step, (i + 1) * step)
        other = far[at, :].astype(F32)
        dk = dkq[at, :GROUP_COLS] + other[:, :GROUP_COLS]
        kq = jnp.concatenate([dk, dkq[at, GROUP_COLS:]], axis=1)
        c3 = jnp.concatenate([cos[at, :]] * 3, axis=1)
        s3 = jnp.concatenate([sin[at, :]] * 3, axis=1)
        low_kq = (kq * c3 - swapped(kq) * s3).astype(BF16)
        low_v = (dv[at, :] + other[:, GROUP_COLS:]).astype(BF16)
        jgkq[at, :] = low_kq
        jgv[at, :] = low_v
        bias_kq += jnp.sum(low_kq.astype(F32), axis=0, keepdims=True)
        bias_v += jnp.sum(low_v.astype(F32), axis=0, keepdims=True)
        first[at, :] = mm_nt(low_kq, w[:, :two]) + mm_nt(low_v, w[:, two:])
    dgain = jnp.zeros((1, width), F32)
    dshift = jnp.zeros((1, width), F32)
    for side in range(2):
        for j in range(GROUPS):
            at = slice((side * GROUPS + j) * half, (side * GROUPS + j + 1) * half)
            mine = slice(side * half, (side + 1) * half)
            norm, _ = normed(xs[j][mine, :].astype(F32))
            grad = first[at, :]
            dgain += jnp.sum(grad * norm, axis=0, keepdims=True)
            dshift += jnp.sum(grad, axis=0, keepdims=True)
            if j == 0:
                ca[mine, :] = grad * gain
            else:
                sends[j - 1][mine, :] = (grad * gain).astype(BF16)
    gsum = jnp.sum(g_own[...].astype(F32), axis=0, keepdims=True)
    dwbuf[:, :two] = mm_tn(fi[...], jgkq[...])
    dwbuf[:, two:] = mm_tn(fi[...], jgv[...])
    ext[...] = jnp.zeros_like(ext)
    for owner in range(GROUPS):
        own = slice(owner * shard, (owner + 1) * shard)
        for slot in range(3):
            unit = owner * 3 + slot
            kind = unit // GROUPS
            vector = (bias_kq[:, GROUP_COLS:], bias_kq[:, :GROUP_COLS], bias_v)[kind]
            to = slice(slot * GROUP_COLS, (slot + 1) * GROUP_COLS)
            ext[owner, 0:1, to] = jnp.where(group == unit % GROUPS, vector, 0.0)
        for slot, vector in enumerate((dgain[:, own], dshift[:, own], gsum[:, own])):
            ext[owner, 1:2, slot * shard : (slot + 1) * shard] = vector
    for k in range(GROUPS):
        owner = z ^ k
        base = owner * shard
        keep[k, 0:part, :] = dwbuf[pl.ds(pl.multiple_of(base + core * part, part), part), :]
        send[k, 0:part, :] = dwbuf[
            pl.ds(pl.multiple_of(base + (1 - core) * part, part), part), :
        ].astype(BF16)
        keep[k, part:, :] = ext[owner].astype(BF16).astype(F32)
        send[k, part:, :] = ext[owner].astype(BF16)


def ffn_pair_body(places, keep, got, c1, c2, c3, own, *sends):
    chunk = own.shape[0]
    for j in range(GROUPS):
        total = keep[j * chunk : (j + 1) * chunk, :] + got[j * chunk : (j + 1) * chunk, :].astype(F32)
        if j == 0:
            own[...] = total
        else:
            sends[j - 1][0:chunk, :] = total.astype(BF16)
            sends[j - 1][chunk:, :] = (c1, c2, c3)[j - 1][...]


def qkv_pair_body(places, keep, got, sums, sums_far, own, *rest):
    sends, ext = rest[:-1], rest[-1]
    z = places[1]
    part = own.shape[0] - EXTRA
    first = sums_far.shape[0] - EXTRA
    vector = sums[...].astype(F32) + sums_far[first:, :].astype(F32)
    shard = vector.shape[1] // GROUPS
    ext[...] = jnp.zeros_like(ext)
    for owner in range(GROUPS):
        at = slice(owner * shard, (owner + 1) * shard)
        here = z == owner
        ext[owner, 2:3, 0:shard] = vector[0:1, at]
        ext[owner, 2:3, shard : 2 * shard] = vector[1:2, at]
        ext[owner, 2:3, 2 * shard : 3 * shard] = jnp.where(here, vector[2:3, 0:shard], 0.0)
        ext[owner, 3:4, :] = jnp.where(here, vector[2:3, shard:], 0.0)
    for k in range(GROUPS):
        total = keep[k] + got[k].astype(F32)
        tail = total[part:, :] + ext[z ^ k]
        if k == 0:
            own[0:part, :] = total[0:part, :]
            own[part:, :] = tail
        else:
            sends[k - 1][0:part, :] = total[0:part, :].astype(BF16)
            sends[k - 1][part:, :] = tail.astype(BF16)


def ffn_sum_body(places, own, a, b, c, qkv, out):
    rows = own.shape[0]
    total = own[...]
    for piece in (a, b, c):
        total += piece[0:rows, :].astype(F32)
    out[0:rows, :] = total.astype(BF16)
    most = qkv.shape[0] - 2 * EXTRA
    block = qkv.shape[1] // 3
    out[rows:, :] = jnp.zeros((out.shape[0] - rows, 4 * block), BF16)
    out[rows : rows + most, 0 : 3 * block] = qkv[0:most, :]
    for i in range(3):
        out[rows + i * EXTRA : rows + (i + 1) * EXTRA, 3 * block :] = qkv[
            most : most + EXTRA, i * block : (i + 1) * block
        ]
    out[rows + most :, 0 : 3 * block] = qkv[most + EXTRA :, :]


def sum_body(places, own, a, b, c, out):
    out[...] = (own[...] + a[...].astype(F32) + b[...].astype(F32) + c[...].astype(F32)).astype(
        out.dtype
    )


def ffn_body(places, *refs):
    line = refs[0:7]
    up_w, down_w, up_b, vec, out_w = refs[7:12]
    atts = refs[12:16]
    outs = refs[16:20]
    sums, si, gb, active, hidden_grad, att = refs[20:26]
    second, norms = refs[26:]
    c, z = places[0], places[1]
    rows = line[0].shape[0] // 2
    width = up_w.shape[0]
    hid = up_w.shape[1]
    gain, shift = vec[2:3, :], vec[3:4, :]
    for k in range(GROUPS):
        at = slice(k * rows, (k + 1) * rows)
        piece = line[0] if k == 0 else line[k][...] + line[7 - k][...]
        norm, _ = normed(piece[0:rows, :].astype(F32))
        norms[at, :] = norm
        si[at, :] = (norm * gain + shift).astype(BF16)
        gb[at, :] = piece[rows:, :]
    for m in range(GROUPS):
        slot = (z - ((c // 2) ^ m)) % GROUPS
        att[pl.ds(pl.multiple_of(slot * rows, rows), rows), :] = atts[m][...]
    step = 2 * rows
    bias_sum = jnp.zeros((1, hid), F32)
    for i in range(GROUPS * rows // step):
        at = slice(i * step, (i + 1) * step)
        hidden = mm(si[at, :], up_w[...]) + up_b[...].astype(F32)
        cdf = 0.5 + 0.5 * lax.erf(hidden * (0.5**0.5))
        density = jnp.exp(hidden * hidden * -0.5) * (1.0 / math.sqrt(2.0 * math.pi))
        active[at, :] = (hidden * cdf).astype(BF16)
        grad = (mm_nt(gb[at, :], down_w[...]) * (cdf + hidden * density)).astype(BF16)
        hidden_grad[at, :] = grad
        bias_sum += jnp.sum(grad.astype(F32), axis=0, keepdims=True)
        part = mm(active[at, :], down_w[...]) + mm(att[at, :], out_w[...])
        second[at, :] = mm_nt(grad, up_w[...])
        for k in range(2):
            piece = outs[2 * i + k]
            piece[0:rows, :] = part[k * rows : (k + 1) * rows, :].astype(piece.dtype)
    dgain = jnp.zeros((1, width), F32)
    dshift = jnp.zeros((1, width), F32)
    for k in range(GROUPS):
        at = slice(k * rows, (k + 1) * rows)
        norm = norms[at, :]
        grad = second[at, :]
        dgain += jnp.sum(grad * norm, axis=0, keepdims=True)
        dshift += jnp.sum(grad, axis=0, keepdims=True)
        outs[k][rows:, :] = (grad * gain).astype(outs[k].dtype)
    row = lax.broadcasted_iota(jnp.int32, sums.shape, 0)
    vectors = jnp.where(row == 0, dgain, jnp.where(row == 1, dshift, bias_sum))
    sums[...] = jnp.where(row < 3, vectors, 0.0).astype(BF16)


def ffn_dw_body(places, si, gb, active, hidden_grad, att, sums, keep, send, dwbuf):
    c = places[0]
    width, hid, shard = si.shape[1], active.shape[1], att.shape[1]
    dwbuf[0:width, :] = mm_tn(si[...], hidden_grad[...])
    dwbuf[width : width + hid, :] = mm_tn(active[...], gb[...])
    dwbuf[width + hid : width + hid + shard, :] = mm_tn(att[...], gb[...])
    dwbuf[width + hid + shard :, :] = jnp.zeros_like(dwbuf[width + hid + shard :, :])
    chunk = dwbuf.shape[0] // (2 * GROUPS)
    for j in range(GROUPS):
        to = slice(j * chunk, (j + 1) * chunk)
        near = c ^ (2 * j)
        keep[to, :] = dwbuf[pl.ds(pl.multiple_of(near * chunk, chunk), chunk), :]
        far = near ^ 1
        send[to, :] = dwbuf[pl.ds(pl.multiple_of(far * chunk, chunk), chunk), :].astype(BF16)
    send[GROUPS * chunk :, :] = sums[...]


def stack_body(places, a, b, c, d, out):
    rows = a.shape[0]
    for j, piece in enumerate((a, b, c, d)):
        out[j * rows : (j + 1) * rows, :] = piece[...]


def spread_body(places, near, far, *refs):
    up_dw, down_dw, out_dw, qkv_dw, vec, up_db, bias, buf, box, qkv_box = refs
    c = places[0]
    core, group = c % 2, c // 2
    shard = out_dw.shape[0]
    part = shard // 2
    rows = near.shape[0] // GROUPS
    chunk = rows - part
    most = part - EXTRA
    three = 3 * GROUP_COLS
    for j in range(GROUPS):
        for side, stack in ((core, near), (1 - core, far)):
            place = 2 * (group ^ j) + side
            base = j * rows
            buf[pl.ds(pl.multiple_of(place * chunk, chunk), chunk), :] = stack[
                base : base + chunk, :
            ].astype(F32)
            base += chunk
            at = pl.multiple_of(side * part, part)
            qkv_box[group ^ j, pl.ds(at, most), :] = stack[base : base + most, 0:three].astype(F32)
            for i in range(3):
                qkv_box[
                    group ^ j,
                    pl.ds(pl.multiple_of(at + most, EXTRA), EXTRA),
                    i * GROUP_COLS : (i + 1) * GROUP_COLS,
                ] = stack[base + i * EXTRA : base + (i + 1) * EXTRA, three:].astype(F32)
        box[group ^ j] = near[j * rows + chunk + most : (j + 1) * rows, 0:three].astype(F32)
    last = up_dw.shape[0] + down_dw.shape[0]
    up_dw[...] = buf[0 : up_dw.shape[0], :]
    down_dw[...] = buf[up_dw.shape[0] : last, :]
    out_dw[...] = buf[last : last + shard, :]
    for g in range(GROUPS):
        for kind, slot in enumerate((1, 0, 2)):
            at = (kind * GROUPS + g) * GROUP_COLS
            qkv_dw[:, at : at + GROUP_COLS] = qkv_box[
                g, :, slot * GROUP_COLS : (slot + 1) * GROUP_COLS
            ]
    total = box[0] + box[1] + box[2] + box[3]
    bias[...] = total[0:1, :]
    for slot in range(3):
        vec[slot : slot + 1, :] = total[1:2, slot * shard : (slot + 1) * shard]
    vec[3:4, :] = total[2:3, 0:shard]
    vec[4:5, :] = total[2:3, shard : 2 * shard]
    up_db[0:1, 0:shard] = total[2:3, 2 * shard :]
    up_db[0:1, shard:] = total[3:4, :]


def token_body(places, xg, vec, ca, ffn, *refs):
    from_plane, from_line = refs[0:3], refs[3:6]
    layer_out, input_grad = refs[6:]
    rows = ca.shape[0]
    values = xg[0:rows, :].astype(F32)
    total = values + vec[4:5, :] + vec[5:6, :] + ffn[0:rows, :]
    cot = ca[...] + ffn[rows:, :]
    for piece in from_plane:
        cot += piece[piece.shape[0] - rows :, :].astype(F32)
    for piece in from_line:
        total += piece[0:rows, :].astype(F32)
        cot += piece[rows:, :].astype(F32)
    layer_out[...] = total.astype(BF16)
    norm, scale = normed(values)
    shifted = cot - jnp.mean(cot, axis=-1, keepdims=True)
    shifted -= norm * jnp.mean(cot * norm, axis=-1, keepdims=True)
    input_grad[...] = xg[rows:, :].astype(F32) + scale * shifted


def block_shards(
    tokens,
    cotangent,
    att_gain,
    att_shift,
    ffn_gain,
    ffn_shift,
    qkv_weight,
    qkv_bias,
    out_weight,
    out_bias,
    up_weight,
    up_bias,
    down_weight,
    down_bias,
):
    width = tokens.shape[-1]
    x = tokens.reshape(-1, width)
    g = cotangent.reshape(-1, width)
    rows = x.shape[0]
    n_ctx, n_z = lax.axis_size("ctx"), lax.axis_size("fsdp")
    c, z = lax.axis_index("ctx"), lax.axis_index("fsdp")
    group = c // 2
    shard = width // n_z
    part = shard // 2
    hid = up_weight.shape[1]
    places = jnp.stack([c, z]).astype(jnp.int32)
    three = 3 * GROUP_COLS
    near_rows = GROUPS * rows
    pair = 2 * rows

    def over_ctx(value, k):
        return lax.ppermute(value, "ctx", [(i, i ^ k) for i in range(n_ctx)])

    def over_z(value, k):
        return lax.ppermute(value, "fsdp", [(i, i ^ k) for i in range(n_z)])

    def around_z(value, k):
        return lax.ppermute(value, "fsdp", [(i, (i + k) % n_z) for i in range(n_z)])

    def along_z(value, k, first):
        pairs = [(i, i + 1) for i in range(first, n_z - 1)]
        if k < 0:
            pairs = [(n_z - 1 - a, n_z - 1 - b) for a, b in pairs]
        return lax.ppermute(value, "fsdp", pairs)

    def over_both(value, pairs):
        return lax.ppermute(
            value, ("ctx", "fsdp"), [(a * n_z + b, d * n_z + e) for a, b, d, e in pairs]
        )

    def chips(value):
        return [value] + [over_ctx(value, 2 * j) for j in range(1, GROUPS)]

    payload, xg, xg_line, out_half = local_call(
        "pack",
        pack_body,
        places,
        [att_gain, att_shift, ffn_gain, ffn_shift, out_bias, down_bias, qkv_bias],
        [((part + EXTRA, three), BF16)] + [((pair, width), BF16)] * 2 + [((part, width), BF16)],
        [
            pltpu.VMEM((EXTRA, three), F32),
            pltpu.VMEM((part, 3 * width), BF16),
            pltpu.SemaphoreType.DMA((6,)),
        ],
        whole=[qkv_weight, x, g, out_weight],
        vmem=60,
    )
    near_w = [payload] + [over_z(payload, k) for k in range(1, n_z)]
    plane = chips(xg)
    by_place = [(a, b, a, b ^ (a // 2)) for a in range(n_ctx) for b in range(n_z)]
    by_plane = [(a, b, a ^ (2 * b), b) for a in range(n_ctx) for b in range(n_z)]
    ow_first = over_both(out_half, by_place)
    ow_near = over_both(ow_first, by_plane)
    stack, vec, bias, xg_line = local_call(
        "collect",
        collect_body,
        places,
        near_w,
        [((GROUPS * part, three), BF16), ((8, width), F32), ((8, three), F32)],
        [pltpu.VMEM((GROUPS, EXTRA, three), F32)],
        after=plane[1:],
        through=[xg_line],
    )
    up, down = [xg_line], [xg_line]
    for i in range(n_z - 1):
        up.append(along_z(up[-1], 1, i))
        down.append(along_z(down[-1], -1, i))
    line = up + down[1:]
    cos_tab, sin_tab = rotary_tables(rows, n_ctx)
    fi, w, q, kv, cos, sin = local_call(
        "qkv",
        qkv_body,
        places,
        [*plane, stack, over_ctx(stack, 1), vec, bias, cos_tab, sin_tab],
        [
            ((near_rows, width), BF16),
            ((width, three), BF16),
            ((near_rows, GROUP_COLS), BF16),
            ((2 * near_rows, GROUP_COLS), BF16),
            ((near_rows, 128), F32),
            ((near_rows, 128), F32),
        ],
        flops=2 * near_rows * width * 4 * GROUP_COLS,
    )
    *att, dkq, dv, far = local_call(
        "attend",
        attend_body,
        places,
        [q, kv, over_ctx(kv, 1), *plane, ow_near, over_ctx(ow_near, 1)],
        [((rows, GROUP_COLS), BF16)] * GROUPS
        + [
            ((near_rows, 2 * GROUP_COLS), F32),
            ((near_rows, GROUP_COLS), F32),
            ((near_rows, 2 * GROUP_COLS), BF16),
        ],
        [
            pltpu.VMEM((2 * near_rows, GROUP_COLS), BF16),
            pltpu.VMEM((2 * near_rows, GROUP_COLS), BF16),
            pltpu.VMEM((near_rows, GROUP_COLS), BF16),
            pltpu.VMEM((near_rows, GROUP_COLS), BF16),
            pltpu.VMEM((GROUP_COLS, width), BF16),
            pltpu.VMEM((near_rows, width), BF16),
            pltpu.VMEM((GROUPS, rows, GROUP_COLS), BF16),
        ],
        flops=2 * 7 * 256 * GROUP_HEADS * near_rows * 2 * near_rows,
    )
    att = [
        over_both(
            att[m], [(a, b, 2 * (b ^ m) + a % 2, a // 2) for a in range(n_ctx) for b in range(n_z)]
        )
        for m in range(GROUPS)
    ]

    ca, *sends, keep, send = local_call(
        "joined",
        joined_body,
        places,
        [dkq, dv, over_ctx(far, 1), w, fi, cos, sin, vec, *plane, g],
        [((rows, width), F32)]
        + [((rows, width), BF16)] * 3
        + [
            ((n_z, part + EXTRA, three), F32),
            ((n_z, part + EXTRA, three), BF16),
        ],
        [
            pltpu.VMEM((near_rows, 2 * GROUP_COLS), BF16),
            pltpu.VMEM((near_rows, GROUP_COLS), BF16),
            pltpu.VMEM((width, three), F32),
            pltpu.VMEM((near_rows, width), F32),
            pltpu.VMEM((GROUPS, EXTRA, three), F32),
        ],
        flops=2 * 2 * near_rows * width * three,
    )
    ca_sends = sends
    chunk = -(-(width + hid + shard) // (n_ctx * EXTRA)) * EXTRA
    *ffn_outs, ffn_sums, si, gb, active, hidden_grad, att = local_call(
        "ffn",
        ffn_body,
        places,
        [*line, up_weight, down_weight, up_bias.reshape(1, -1), vec, out_weight, *att],
        [((pair, width), F32)]
        + [((pair, width), BF16)] * 3
        + [((EXTRA, width), BF16)]
        + [((near_rows, n), BF16) for n in (width, width, hid, hid, GROUP_COLS)],
        [pltpu.VMEM((near_rows, width), F32), pltpu.VMEM((near_rows, width), F32)],
        flops=2 * 4 * near_rows * width * hid,
        after=[keep],
    )
    ffn_keep, ffn_send = local_call(
        "ffn_dw",
        ffn_dw_body,
        places,
        [si, gb, active, hidden_grad, att, ffn_sums],
        [((GROUPS * chunk, width), F32), ((GROUPS * chunk + EXTRA, width), BF16)],
        [pltpu.VMEM((n_ctx * chunk, width), F32)],
        flops=2 * 2 * near_rows * width * hid,
    )

    ffn_far = over_ctx(ffn_send, 1)
    own_qkv, *sends = local_call(
        "qkv_pair",
        qkv_pair_body,
        places,
        [keep, over_ctx(send, 1), ffn_sums, ffn_far],
        [((part + EXTRA, three), F32)] + [((part + EXTRA, three), BF16)] * 3,
        [pltpu.VMEM((GROUPS, EXTRA, three), F32)],
    )
    qkv_total, *line_sends = local_call(
        "qkv_sum",
        sum_body,
        places,
        [own_qkv] + [over_z(sends[k - 1], k) for k in range(1, n_z)],
        [((part + EXTRA, three), BF16)],
        through=ffn_outs[1:],
    )
    from_line = [around_z(line_sends[k - 1], -k) for k in range(1, n_z)]
    own, *sends = local_call(
        "ffn_pair",
        ffn_pair_body,
        places,
        [ffn_keep, ffn_far, *ca_sends],
        [((chunk, width), F32)] + [((chunk + rows, width), BF16)] * 3,
    )
    from_plane = [over_ctx(sends[j - 1], 2 * j) for j in range(1, GROUPS)]
    (ffn_total,) = local_call(
        "plane_share",
        ffn_sum_body,
        places,
        [own, *from_plane, qkv_total],
        [((chunk + part, width), BF16)],
    )
    (near,) = local_call(
        "stack",
        stack_body,
        places,
        chips(ffn_total),
        [((GROUPS * (chunk + part), width), BF16)],
        after=from_line,
    )
    up_dw, down_dw, out_dw, qkv_dw, sums, up_db, qkv_db = local_call(
        "spread",
        spread_body,
        places,
        [near, over_ctx(near, 1)],
        [
            ((width, hid), F32),
            ((hid, width), F32),
            ((shard, width), F32),
            ((shard, 3 * width), F32),
            ((8, shard), F32),
            ((1, hid), F32),
            ((1, three), F32),
        ],
        [
            pltpu.VMEM((n_ctx * chunk, width), F32),
            pltpu.VMEM((GROUPS, EXTRA, three), F32),
            pltpu.VMEM((GROUPS, shard, three), F32),
        ],
        vmem=36,
    )

    layer_out, input_grad = local_call(
        "token",
        token_body,
        places,
        [xg, vec, ca, ffn_outs[0], *from_plane, *from_line],
        [((rows, width), BF16), ((rows, width), F32)],
        after=[near],
    )
    return (
        layer_out.reshape(tokens.shape),
        input_grad.reshape(tokens.shape),
        sums[0],
        sums[1],
        sums[3],
        sums[4],
        qkv_dw,
        qkv_db[0],
        out_dw,
        sums[2],
        up_dw,
        up_db[0],
        down_dw,
        sums[2],
    )


def solution(mesh):
    in_specs = (
        P("fsdp", "ctx", None),
        P("fsdp", "ctx", None),
        P("fsdp"),
        P("fsdp"),
        P("fsdp"),
        P("fsdp"),
        P("fsdp", None),
        P("fsdp"),
        P("fsdp", None),
        P("fsdp"),
        P(None, "fsdp"),
        P("fsdp"),
        P("fsdp", None),
        P("fsdp"),
    )
    out_specs = (
        P("fsdp", "ctx", None),
        P("fsdp", "ctx", None),
        P("fsdp"),
        P("fsdp"),
        P("fsdp"),
        P("fsdp"),
        P("fsdp", None),
        P("fsdp"),
        P("fsdp", None),
        P("fsdp"),
        P(None, "fsdp"),
        P("fsdp"),
        P("fsdp", None),
        P("fsdp"),
    )
    per_device = block_shards if fits(mesh) else shards
    return jax.shard_map(per_device, mesh=mesh, in_specs=in_specs, out_specs=out_specs, check_vma=False)
```

profile of v0, /device:TPU:0, one launch (start us, length us, event | category | flops | bytes accessed | tf_op | source)
XLA Modules:
  0.0 182.7 jit_solution(8088521082854354013)
XLA Ops:
  1.2 3.3 %pack.1 = (bf16[112,576]{1,0:T(8,128)(2,1)}, bf16[256,768]{1,0:T(8,128)(2,1)}, bf16[256,768]{1,0:T(8,128)(2,1)}, bf16[96,768]{1,0:T(8,128)(2,1)}) custom-call(s32[2]{0:T(128)} %pad_add_fusion.refs_0_, bf16[192,768]{1,0:T(8,128)(2,1)} %refs_6_.3, bf16[128,768]{1,0:T(8,128)(2,1)} %bitcast.11, bf16[128,768]{1,0:T(8,128)(2,1)} %bitcast.13, ...), custom_call_target="tpu_custom_call" | custom-call | bytes 1066368 | tf_op jit(solution)/shard_map/pack/pallas_call | solution.py:452
  4.5 3.0 %collective-permute-start.2 = (bf16[256,768]{1,0:T(8,128)(2,1)}, bf16[256,768]{1,0:T(8,128)(2,1)S(1)}, u32[]{:S(2)}, u32[]{:S(2)}) collective-permute-start(bf16[256,768]{1,0:T(8,128)(2,1)} %get-tuple-element.74.refs_10_.refs_6_.refs_5_.refs_11_), channel_id=1, source_target_pairs={{0,8},{4,12},{8,0},{12,4},{16,24},{20,28},{24,16},{28,20},{1,9},{5... | collective-permute-start | bytes 1179656 | tf_op jit(solution)/shard_map/ppermute | solution.py:1020
  7.5 1.5 collective-permute-start.1
  9.1 2.0 %collective-permute-start.5 = (bf16[112,576]{1,0:T(8,128)(2,1)}, bf16[112,576]{1,0:T(8,128)(2,1)S(1)}, u32[]{:S(2)}, u32[]{:S(2)}) collective-permute-start(bf16[112,576]{1,0:T(8,128)(2,1)} %get-tuple-element.76.refs_8_), channel_id=1, source_target_pairs={{0,1},{1,0},{2,3},{3,2},{4,5},{5,4},{6,7},{7,6},{8,9},{9,8},{10,11... | collective-permute-start | bytes 387080 | tf_op jit(solution)/shard_map/ppermute | solution.py:1023
  11.1 2.6 %collective-permute-start.4 = (bf16[112,576]{1,0:T(8,128)(2,1)}, bf16[112,576]{1,0:T(8,128)(2,1)S(1)}, u32[]{:S(2)}, u32[]{:S(2)}) collective-permute-start(bf16[112,576]{1,0:T(8,128)(2,1)} %get-tuple-element.76.refs_8_), channel_id=1, source_target_pairs={{0,2},{1,3},{2,0},{3,1},{4,6},{5,7},{6,4},{7,5},{8,10},{9,11},{10,... | collective-permute-start | bytes 387080 | tf_op jit(solution)/shard_map/ppermute | solution.py:1023
  13.7 2.3 %collective-permute-done.5.refs_7_ = bf16[112,576]{1,0:T(8,128)(2,1)S(1)} collective-permute-done((bf16[112,576]{1,0:T(8,128)(2,1)}, bf16[112,576]{1,0:T(8,128)(2,1)S(1)}, u32[]{:S(2)}, u32[]{:S(2)}) %collective-permute-start.5) | collective-permute-done | bytes 129056 | tf_op jit(solution)/shard_map/ppermute | solution.py:1023
  16.0 4.2 %collective-permute-start.3 = (bf16[112,576]{1,0:T(8,128)(2,1)}, bf16[112,576]{1,0:T(8,128)(2,1)S(1)}, u32[]{:S(2)}, u32[]{:S(2)}) collective-permute-start(bf16[112,576]{1,0:T(8,128)(2,1)} %get-tuple-element.76.refs_8_), channel_id=1, source_target_pairs={{0,3},{1,2},{2,1},{3,0},{4,7},{5,6},{6,5},{7,4},{8,11},{9,10},{10,... | collective-permute-start | bytes 387080 | tf_op jit(solution)/shard_map/ppermute | solution.py:1023
  20.2 1.8 collective-permute-done.4.refs_6_
  22.0 1.6 collective-permute-done.3.refs_5_
  23.6 3.1 %collective-permute-done.1.refs_2_.refs_8_.refs_4_.refs_3_ = bf16[256,768]{1,0:T(8,128)(2,1)S(1)} collective-permute-done((bf16[256,768]{1,0:T(8,128)(2,1)}, bf16[256,768]{1,0:T(8,128)(2,1)S(1)}, u32[]{:S(2)}, u32[]{:S(2)}) %collective-permute-start.1) | collective-permute-done | bytes 393248 | tf_op jit(solution)/shard_map/ppermute | solution.py:1020
  26.7 1.0 copy-done.4
  27.7 0.9 copy-done.8
  29.2 0.8 collect.1
  30.8 3.5 %collective-permute-start.19 = (bf16[256,768]{1,0:T(8,128)(2,1)S(1)}, bf16[256,768]{1,0:T(8,128)(2,1)S(1)}, u32[]{:S(2)}, u32[]{:S(2)}) collective-permute-start(bf16[256,768]{1,0:T(8,128)(2,1)S(1)} %get-tuple-element.95.refs_17_), channel_id=1, source_target_pairs={{0,1},{1,2},{2,3},{4,5},{5,6},{6,7},{8,9},{9,10},{10,11},{12,13},{... | collective-permute-start | bytes 1179656 | tf_op jit(solution)/shard_map/ppermute | solution.py:1032
  34.3 1.3 collective-permute-start.16
  35.7 2.0 %qkv.1 = (bf16[512,768]{1,0:T(8,128)(2,1)S(1)}, bf16[768,576]{1,0:T(8,128)(2,1)S(1)}, bf16[512,192]{1,0:T(8,128)(2,1)S(1)}, bf16[1024,192]{1,0:T(8,128)(2,1)S(1)...) custom-call(s32[2]{0:T(128)S(1)} %copy-done.9, f32[1024,128]{1,0:T(8,128)S(1)} %copy-done.3, f32[1024,128]{1,0:T(8,128)S(1)} %copy-done.2, ...), custom_call_target="tpu_custom_call" | custom-call | flops 603979776 | bytes 6334464 | tf_op jit(solution)/shard_map/qkv/pallas_call | solution.py:452
  39.0 4.2 %collective-permute-done.19.refs_16_ = bf16[256,768]{1,0:T(8,128)(2,1)S(1)} collective-permute-done((bf16[256,768]{1,0:T(8,128)(2,1)S(1)}, bf16[256,768]{1,0:T(8,128)(2,1)S(1)}, u32[]{:S(2)}, u32[]{:S(2)}) %collective-permute-start.19) | collective-permute-done | bytes 393248 | tf_op jit(solution)/shard_map/ppermute | solution.py:1032
  43.9 3.5 %collective-permute-done.16.refs_13_ = bf16[256,768]{1,0:T(8,128)(2,1)S(1)} collective-permute-done((bf16[256,768]{1,0:T(8,128)(2,1)S(1)}, bf16[256,768]{1,0:T(8,128)(2,1)S(1)}, u32[]{:S(2)}, u32[]{:S(2)}) %collective-permute-start.16) | collective-permute-done | bytes 393248 | tf_op jit(solution)/shard_map/ppermute | solution.py:1032
  47.4 1.3 collective-permute-start.17
  48.7 8.0 %attend.1 = (bf16[128,192]{1,0:T(8,128)(2,1)S(1)}, bf16[128,192]{1,0:T(8,128)(2,1)S(1)}, bf16[128,192]{1,0:T(8,128)(2,1)S(1)}, bf16[128,192]{1,0:T(8,128)(2,1)S(...) custom-call(s32[2]{0:T(128)S(1)} %copy-done.9, ...), custom_call_target="tpu_custom_call" | custom-call | flops 5637144576 | bytes 4620288 | tf_op jit(solution)/shard_map/attend/pallas_call | solution.py:452
  57.5 8.0 %collective-permute-done.17.refs_12_ = bf16[256,768]{1,0:T(8,128)(2,1)S(1)} collective-permute-done((bf16[256,768]{1,0:T(8,128)(2,1)S(1)}, bf16[256,768]{1,0:T(8,128)(2,1)S(1)}, u32[]{:S(2)}, u32[]{:S(2)}) %collective-permute-start.17) | collective-permute-done | bytes 393248 | tf_op jit(solution)/shard_map/ppermute | solution.py:1032
  65.5 1.3 collective-permute-start.18
  66.8 1.8 collective-permute-start.12
  68.6 2.6 %collective-permute-start.13 = (bf16[128,192]{1,0:T(8,128)(2,1)S(1)}, bf16[128,192]{1,0:T(8,128)(2,1)S(1)}, u32[]{:S(2)}, u32[]{:S(2)}) collective-permute-start(bf16[128,192]{1,0:T(8,128)(2,1)S(1)} %get-tuple-element.92), channel_id=1, source_target_pairs={{0,16},{1,24},{2,0},{3,8},{4,20},{5,28},{6,4},{7,12},{8,17},{9,25}... | collective-permute-start | bytes 147464 | tf_op jit(solution)/shard_map/ppermute | solution.py:1035
  71.2 1.9 %collective-permute-done.12.refs_2_ = bf16[128,192]{1,0:T(8,128)(2,1)S(1)} collective-permute-done((bf16[128,192]{1,0:T(8,128)(2,1)S(1)}, bf16[128,192]{1,0:T(8,128)(2,1)S(1)}, u32[]{:S(2)}, u32[]{:S(2)}) %collective-permute-start.12) | collective-permute-done | bytes 49184 | tf_op jit(solution)/shard_map/ppermute | solution.py:1035
  73.1 3.6 %collective-permute-start.14 = (bf16[128,192]{1,0:T(8,128)(2,1)S(1)}, bf16[128,192]{1,0:T(8,128)(2,1)S(1)}, u32[]{:S(2)}, u32[]{:S(2)}) collective-permute-start(bf16[128,192]{1,0:T(8,128)(2,1)S(1)} %get-tuple-element.93), channel_id=1, source_target_pairs={{0,8},{1,0},{2,24},{3,16},{4,12},{5,4},{6,28},{7,20},{8,9},{9,1},{... | collective-permute-start | bytes 147464 | tf_op jit(solution)/shard_map/ppermute | solution.py:1035
  76.7 0.8 collective-permute-start.15
  77.6 2.6 %joined.1 = (f32[128,768]{1,0:T(8,128)S(1)}, bf16[128,768]{1,0:T(8,128)(2,1)S(1)}, bf16[128,768]{1,0:T(8,128)(2,1)S(1)}, bf16[128,768]{1,0:T(8,128)(2,1)S(1)}, f...) custom-call(s32[2]{0:T(128)S(1)} %copy-done.9, bf16[128,768]{1,0:T(8,128)(2,1)S(1)} %bitcast.12, ...), custom_call_target="tpu_custom_call" | custom-call | flops 905969664 | bytes 8093696 | tf_op jit(solution)/shard_map/joined/pallas_call | solution.py:452
  80.2 9.9 %collective-permute-done.14.refs_4_ = bf16[128,192]{1,0:T(8,128)(2,1)S(1)} collective-permute-done((bf16[128,192]{1,0:T(8,128)(2,1)S(1)}, bf16[128,192]{1,0:T(8,128)(2,1)S(1)}, u32[]{:S(2)}, u32[]{:S(2)}) %collective-permute-start.14) | collective-permute-done | bytes 49184 | tf_op jit(solution)/shard_map/ppermute | solution.py:1035
  90.1 3.9 %ffn.1 = (f32[256,768]{1,0:T(8,128)S(1)}, bf16[256,768]{1,0:T(8,128)(2,1)S(1)}, bf16[256,768]{1,0:T(8,128)(2,1)S(1)}, bf16[256,768]{1,0:T(8,128)(2,1)S(1)}, bf16...) custom-call(s32[2]{0:T(128)S(1)} %copy-done.9, ...), custom_call_target="tpu_custom_call" | custom-call | flops 2415919104 | bytes 10962432 | tf_op jit(solution)/shard_map/ffn/pallas_call | solution.py:452
  94.0 2.5 %ffn_dw.1 = (f32[896,768]{1,0:T(8,128)S(1)}, bf16[912,768]{1,0:T(8,128)(2,1)S(1)}) custom-call(s32[2]{0:T(128)S(1)} %copy-done.9, bf16[16,768]{1,0:T(8,128)(2,1)S(1)} %get-tuple-element.99.refs_1_.refs_2_, bf16[512,192]{1,0:T(8,128)(2,1)S(1)} %get-tuple-element.100.refs_2_, bf16[512,768]{1,0:T(8,128)(2,1)S(1)} %get-tuple-element.101.refs_3_, ...), custom_call_target="tpu_custom_call" | custom-call | flops 1207959552 | bytes 7520256 | tf_op jit(solution)/shard_map/ffn_dw/pallas_call | solution.py:452
  97.1 3.5 %collective-permute-done.23.refs_3_ = bf16[4,112,576]{2,1,0:T(8,128)(2,1)S(1)} collective-permute-done((bf16[4,112,576]{2,1,0:T(8,128)(2,1)S(1)}, bf16[4,112,576]{2,1,0:T(8,128)(2,1)S(1)}, u32[]{:S(2)}, u32[]{:S(2)}) %collective-permute-start.23) | collective-permute-done | bytes 516128 | tf_op jit(solution)/shard_map/ppermute | solution.py:1020
  101.3 12.3 %collective-permute-start.24 = (bf16[112,576]{1,0:T(8,128)(2,1)S(1)}, bf16[112,576]{1,0:T(8,128)(2,1)S(1)}, u32[]{:S(2)}, u32[]{:S(2)}) collective-permute-start(bf16[112,576]{1,0:T(8,128)(2,1)S(1)} %get-tuple-element.107), channel_id=1, source_target_pairs={{0,3},{1,2},{2,1},{3,0},{4,7},{5,6},{6,5},{7,4},{8,11},{9,10},{10,... | collective-permute-start | bytes 387080 | tf_op jit(solution)/shard_map/ppermute | solution.py:1023
  113.6 0.9 ffn_pair.1
  114.6 3.4 %collective-permute-start.32 = (bf16[352,768]{1,0:T(8,128)(2,1)S(1)}, bf16[352,768]{1,0:T(8,128)(2,1)S(1)}, u32[]{:S(2)}, u32[]{:S(2)}) collective-permute-start(bf16[352,768]{1,0:T(8,128)(2,1)S(1)} %get-tuple-element.121), channel_id=1, source_target_pairs={{0,8},{4,12},{8,0},{12,4},{16,24},{20,28},{24,16},{28,20},{1,9},{5... | collective-permute-start | bytes 1622024 | tf_op jit(solution)/shard_map/ppermute | solution.py:1020
  118.6 5.8 %collective-permute-done.25.refs_5_ = bf16[112,576]{1,0:T(8,128)(2,1)S(1)} collective-permute-done((bf16[112,576]{1,0:T(8,128)(2,1)S(1)}, bf16[112,576]{1,0:T(8,128)(2,1)S(1)}, u32[]{:S(2)}, u32[]{:S(2)}) %collective-permute-start.25) | collective-permute-done | bytes 129056 | tf_op jit(solution)/shard_map/ppermute | solution.py:1023
  124.4 1.6 collective-permute-done.26.refs_6_
  126.6 2.7 %collective-permute-start.27 = (bf16[256,768]{1,0:T(8,128)(2,1)S(1)}, bf16[256,768]{1,0:T(8,128)(2,1)S(1)}, u32[]{:S(2)}, u32[]{:S(2)}) collective-permute-start(bf16[256,768]{1,0:T(8,128)(2,1)S(1)} %get-tuple-element.111), channel_id=1, source_target_pairs={{0,3},{1,0},{2,1},{3,2},{4,7},{5,4},{6,5},{7,6},{8,11},{9,8},{10,9... | collective-permute-start | bytes 1179656 | tf_op jit(solution)/shard_map/ppermute | solution.py:1026
  129.3 1.3 collective-permute-done.30.refs_2_.refs_5_
  130.6 9.6 %collective-permute-done.31.refs_3_.refs_6_ = bf16[352,768]{1,0:T(8,128)(2,1)S(1)} collective-permute-done((bf16[352,768]{1,0:T(8,128)(2,1)S(1)}, bf16[352,768]{1,0:T(8,128)(2,1)S(1)}, u32[]{:S(2)}, u32[]{:S(2)}) %collective-permute-start.31) | collective-permute-done | bytes 540704 | tf_op jit(solution)/shard_map/ppermute | solution.py:1020
  140.2 0.8 plane_share.1.refs_7_
  141.4 1.4 collective-permute-start.34
  142.8 1.8 collective-permute-start.33
  144.6 1.7 collective-permute-start.29
  146.3 24.7 %collective-permute-done.28.refs_2_.refs_3_ = bf16[256,768]{1,0:T(8,128)(2,1)S(1)} collective-permute-done((bf16[256,768]{1,0:T(8,128)(2,1)S(1)}, bf16[256,768]{1,0:T(8,128)(2,1)S(1)}, u32[]{:S(2)}, u32[]{:S(2)}) %collective-permute-start.28) | collective-permute-done | bytes 393248 | tf_op jit(solution)/shard_map/ppermute | solution.py:1026
  171.8 1.8 token_.1
  173.6 2.1 %collective-permute-done.36.refs_1_ = bf16[1280,768]{1,0:T(8,128)(2,1)S(1)} collective-permute-done((bf16[1280,768]{1,0:T(8,128)(2,1)S(1)}, bf16[1280,768]{1,0:T(8,128)(2,1)S(1)}, u32[]{:S(2)}, u32[]{:S(2)}) %collective-permute-start.36) | collective-permute-done | bytes 1966112 | tf_op jit(solution)/shard_map/ppermute | solution.py:1020
  175.8 4.5 %spread.1 = (f32[768,768]{1,0:T(8,128)}, f32[768,768]{1,0:T(8,128)}, f32[192,768]{1,0:T(8,128)}, f32[192,2304]{1,0:T(8,128)}, f32[8,192]{1,0:T(8,128)S(1)}, /*index=5*/f32[1,768]{1,0:T(1,128)S(1)}, f32[1,576]{1,0:T(1,128)S(1)}) custom-call(s32[2]{0:T(128)S(1)} %copy-done.10, bf16[1280,768]{1,0:T(8,128)(2,1)S(1)} %collective-permute-done.36.refs_1_, ...), custom_call_target="tpu_custom_call" | custom-call | bytes 11021568 | tf_op jit(solution)/shard_map/spread/pallas_call | solution.py:452
  (78 shorter events, 10.9 us)
Async XLA Ops:
  1.2 34.4 %copy-start.2 = (f32[1024,128]{1,0:T(8,128)S(1)}, f32[1024,128]{1,0:T(8,128)}, u32[]{:S(2)}) copy-start(f32[1024,128]{1,0:T(8,128)} %constant.14.clone.refs_2_) | copy-start | bytes 1572868
  1.2 34.4 %copy-start.3 = (f32[1024,128]{1,0:T(8,128)S(1)}, f32[1024,128]{1,0:T(8,128)}, u32[]{:S(2)}) copy-start(f32[1024,128]{1,0:T(8,128)} %constant.13.clone.refs_1_) | copy-start | bytes 1572868
  4.5 31.2 %copy-start = (bf16[256,768]{1,0:T(8,128)(2,1)S(1)}, bf16[256,768]{1,0:T(8,128)(2,1)}, u32[]{:S(2)}) copy-start(bf16[256,768]{1,0:T(8,128)(2,1)} %get-tuple-element.74.refs_10_.refs_6_.refs_5_.refs_11_) | copy-start | bytes 1179652
  4.5 19.1 %collective-permute-start.2 = (bf16[256,768]{1,0:T(8,128)(2,1)}, bf16[256,768]{1,0:T(8,128)(2,1)S(1)}, u32[]{:S(2)}, u32[]{:S(2)}) collective-permute-start(bf16[256,768]{1,0:T(8,128)(2,1)} %get-tuple-element.74.refs_10_.refs_6_.refs_5_.refs_11_), channel_id=1, source_target_pairs={{0,8},{4,12},{8,0},{12,4},{16,24},{20,28},{24,16},{28,20},{1,9},{5... | collective-permute-start | bytes 1179656 | tf_op jit(solution)/shard_map/ppermute | solution.py:1020
  7.5 19.2 %collective-permute-start.1 = (bf16[256,768]{1,0:T(8,128)(2,1)}, bf16[256,768]{1,0:T(8,128)(2,1)S(1)}, u32[]{:S(2)}, u32[]{:S(2)}) collective-permute-start(bf16[256,768]{1,0:T(8,128)(2,1)} %get-tuple-element.74.refs_10_.refs_6_.refs_5_.refs_11_), channel_id=1, source_target_pairs={{0,16},{4,20},{8,24},{12,28},{16,0},{20,4},{24,8},{28,12},{1,17},{... | collective-permute-start | bytes 1179656 | tf_op jit(solution)/shard_map/ppermute | solution.py:1020
  9.0 17.6 %collective-permute-start = (bf16[256,768]{1,0:T(8,128)(2,1)}, bf16[256,768]{1,0:T(8,128)(2,1)S(1)}, u32[]{:S(2)}, u32[]{:S(2)}) collective-permute-start(bf16[256,768]{1,0:T(8,128)(2,1)} %get-tuple-element.74.refs_10_.refs_6_.refs_5_.refs_11_), channel_id=1, source_target_pairs={{0,24},{4,28},{8,16},{12,20},{16,8},{20,12},{24,0},{28,4},{1,25},{... | collective-permute-start | bytes 1179656 | tf_op jit(solution)/shard_map/ppermute | solution.py:1020
  9.1 6.9 %collective-permute-start.5 = (bf16[112,576]{1,0:T(8,128)(2,1)}, bf16[112,576]{1,0:T(8,128)(2,1)S(1)}, u32[]{:S(2)}, u32[]{:S(2)}) collective-permute-start(bf16[112,576]{1,0:T(8,128)(2,1)} %get-tuple-element.76.refs_8_), channel_id=1, source_target_pairs={{0,1},{1,0},{2,3},{3,2},{4,5},{5,4},{6,7},{7,6},{8,9},{9,8},{10,11... | collective-permute-start | bytes 387080 | tf_op jit(solution)/shard_map/ppermute | solution.py:1023
  11.1 10.9 %collective-permute-start.4 = (bf16[112,576]{1,0:T(8,128)(2,1)}, bf16[112,576]{1,0:T(8,128)(2,1)S(1)}, u32[]{:S(2)}, u32[]{:S(2)}) collective-permute-start(bf16[112,576]{1,0:T(8,128)(2,1)} %get-tuple-element.76.refs_8_), channel_id=1, source_target_pairs={{0,2},{1,3},{2,0},{3,1},{4,6},{5,7},{6,4},{7,5},{8,10},{9,11},{10,... | collective-permute-start | bytes 387080 | tf_op jit(solution)/shard_map/ppermute | solution.py:1023
  16.0 7.6 %collective-permute-start.3 = (bf16[112,576]{1,0:T(8,128)(2,1)}, bf16[112,576]{1,0:T(8,128)(2,1)S(1)}, u32[]{:S(2)}, u32[]{:S(2)}) collective-permute-start(bf16[112,576]{1,0:T(8,128)(2,1)} %get-tuple-element.76.refs_8_), channel_id=1, source_target_pairs={{0,3},{1,2},{2,1},{3,0},{4,7},{5,6},{6,5},{7,4},{8,11},{9,10},{10,... | collective-permute-start | bytes 387080 | tf_op jit(solution)/shard_map/ppermute | solution.py:1023
  30.0 7.7 %copy-start.5 = (bf16[256,768]{1,0:T(8,128)(2,1)}, bf16[256,768]{1,0:T(8,128)(2,1)S(1)}, u32[]{:S(2)}) copy-start(bf16[256,768]{1,0:T(8,128)(2,1)S(1)} %get-tuple-element.95.refs_17_) | copy-start | bytes 1179652
  30.0 5.6 %collective-permute-start.6 = (bf16[384,576]{1,0:T(8,128)(2,1)S(1)}, bf16[384,576]{1,0:T(8,128)(2,1)S(1)}, u32[]{:S(2)}, u32[]{:S(2)}) collective-permute-start(bf16[384,576]{1,0:T(8,128)(2,1)S(1)} %get-tuple-element.79.refs_6_), channel_id=1, source_target_pairs={{0,4},{4,0},{8,12},{12,8},{16,20},{20,16},{24,28},{28,24},{1,5},{5... | collective-permute-start | bytes 1327112 | tf_op jit(solution)/shard_map/ppermute | solution.py:1020
  30.1 7.8 %collective-permute-start.7 = (bf16[96,768]{1,0:T(8,128)(2,1)S(1)}, bf16[96,768]{1,0:T(8,128)(2,1)S(1)}, u32[]{:S(2)}, u32[]{:S(2)}) collective-permute-start(bf16[96,768]{1,0:T(8,128)(2,1)S(1)} %copy-done.15), channel_id=1, source_target_pairs={{0,0},{1,1},{2,2},{3,3},{4,4},{5,5},{6,6},{7,7},{8,9},{9,8},{10,11... | collective-permute-start | bytes 442376 | tf_op jit(solution)/shard_map/ppermute | solution.py:1035
  30.8 12.5 %collective-permute-start.19 = (bf16[256,768]{1,0:T(8,128)(2,1)S(1)}, bf16[256,768]{1,0:T(8,128)(2,1)S(1)}, u32[]{:S(2)}, u32[]{:S(2)}) collective-permute-start(bf16[256,768]{1,0:T(8,128)(2,1)S(1)} %get-tuple-element.95.refs_17_), channel_id=1, source_target_pairs={{0,1},{1,2},{2,3},{4,5},{5,6},{6,7},{8,9},{9,10},{10,11},{12,13},{... | collective-permute-start | bytes 1179656 | tf_op jit(solution)/shard_map/ppermute | solution.py:1032
  34.3 13.1 %collective-permute-start.16 = (bf16[256,768]{1,0:T(8,128)(2,1)S(1)}, bf16[256,768]{1,0:T(8,128)(2,1)S(1)}, u32[]{:S(2)}, u32[]{:S(2)}) collective-permute-start(bf16[256,768]{1,0:T(8,128)(2,1)S(1)} %get-tuple-element.95.refs_17_), channel_id=1, source_target_pairs={{3,2},{2,1},{1,0},{7,6},{6,5},{5,4},{11,10},{10,9},{9,8},{15,14},{... | collective-permute-start | bytes 1179656 | tf_op jit(solution)/shard_map/ppermute | solution.py:1032
  37.7 11.0 %collective-permute-start.10 = (bf16[1024,192]{1,0:T(8,128)(2,1)S(1)}, bf16[1024,192]{1,0:T(8,128)(2,1)S(1)}, u32[]{:S(2)}, u32[]{:S(2)}) collective-permute-start(bf16[1024,192]{1,0:T(8,128)(2,1)S(1)} %get-tuple-element.85.refs_8_), channel_id=1, source_target_pairs={{0,4},{4,0},{8,12},{12,8},{16,20},{20,16},{24,28},{28,24},{1,5},{5... | collective-permute-start | bytes 1179656 | tf_op jit(solution)/shard_map/ppermute | solution.py:1020
  37.9 0.7 collective-permute-start.8
  38.6 10.1 %collective-permute-start.9 = (bf16[96,768]{1,0:T(8,128)(2,1)S(1)}, bf16[96,768]{1,0:T(8,128)(2,1)S(1)}, u32[]{:S(2)}, u32[]{:S(2)}) collective-permute-start(bf16[96,768]{1,0:T(8,128)(2,1)S(1)} %collective-permute-done.8.refs_2_), channel_id=1, source_target_pairs={{0,4},{4,0},{8,12},{12,8},{16,20},{20,16},{24,28},{28,24},{1,5},{5... | collective-permute-start | bytes 442376 | tf_op jit(solution)/shard_map/ppermute | solution.py:1020
  43.3 13.5 %collective-permute-start.20 = (bf16[256,768]{1,0:T(8,128)(2,1)S(1)}, bf16[256,768]{1,0:T(8,128)(2,1)S(1)}, u32[]{:S(2)}, u32[]{:S(2)}) collective-permute-start(bf16[256,768]{1,0:T(8,128)(2,1)S(1)} %collective-permute-done.19.refs_16_), channel_id=1, source_target_pairs={{1,2},{2,3},{5,6},{6,7},{9,10},{10,11},{13,14},{14,15},{17,18},{18... | collective-permute-start | bytes 1179656 | tf_op jit(solution)/shard_map/ppermute | solution.py:1032
  47.4 18.1 %collective-permute-start.17 = (bf16[256,768]{1,0:T(8,128)(2,1)S(1)}, bf16[256,768]{1,0:T(8,128)(2,1)S(1)}, u32[]{:S(2)}, u32[]{:S(2)}) collective-permute-start(bf16[256,768]{1,0:T(8,128)(2,1)S(1)} %collective-permute-done.16.refs_13_), channel_id=1, source_target_pairs={{2,1},{1,0},{6,5},{5,4},{10,9},{9,8},{14,13},{13,12},{18,17},{17,1... | collective-permute-start | bytes 1179656 | tf_op jit(solution)/shard_map/ppermute | solution.py:1032
  48.7 19.9 %copy-start.14 = (bf16[768]{0:T(1024)(128)(2,1)S(1)}, bf16[768]{0:T(1024)(128)(2,1)}, u32[]{:S(2)}) copy-start(bf16[768]{0:T(1024)(128)(2,1)} %param.27) | copy-start | bytes 4612
  48.7 28.8 %copy-start.1 = (bf16[1,128,768]{2,1,0:T(8,128)(2,1)S(1)}, bf16[1,128,768]{2,1,0:T(8,128)(2,1)}, u32[]{:S(2)}) copy-start(bf16[1,128,768]{2,1,0:T(8,128)(2,1)} %param.17) | copy-start | bytes 589828
  56.7 20.0 %collective-permute-start.11 = (bf16[512,384]{1,0:T(8,128)(2,1)S(1)}, bf16[512,384]{1,0:T(8,128)(2,1)S(1)}, u32[]{:S(2)}, u32[]{:S(2)}) collective-permute-start(bf16[512,384]{1,0:T(8,128)(2,1)S(1)} %get-tuple-element.87), channel_id=1, source_target_pairs={{0,4},{4,0},{8,12},{12,8},{16,20},{20,16},{24,28},{28,24},{1,5},{5... | collective-permute-start | bytes 1179656 | tf_op jit(solution)/shard_map/ppermute | solution.py:1020
  56.8 33.3 %collective-permute-start.21 = (bf16[256,768]{1,0:T(8,128)(2,1)S(1)}, bf16[256,768]{1,0:T(8,128)(2,1)S(1)}, u32[]{:S(2)}, u32[]{:S(2)}) collective-permute-start(bf16[256,768]{1,0:T(8,128)(2,1)S(1)} %collective-permute-done.20.refs_15_), channel_id=1, source_target_pairs={{2,3},{6,7},{10,11},{14,15},{18,19},{22,23},{26,27},{30,31}} | collective-permute-start | bytes 1179656 | tf_op jit(solution)/shard_map/ppermute | solution.py:1032
  65.5 24.6 %collective-permute-start.18 = (bf16[256,768]{1,0:T(8,128)(2,1)S(1)}, bf16[256,768]{1,0:T(8,128)(2,1)S(1)}, u32[]{:S(2)}, u32[]{:S(2)}) collective-permute-start(bf16[256,768]{1,0:T(8,128)(2,1)S(1)} %collective-permute-done.17.refs_12_), channel_id=1, source_target_pairs={{1,0},{5,4},{9,8},{13,12},{17,16},{21,20},{25,24},{29,28}} | collective-permute-start | bytes 1179656 | tf_op jit(solution)/shard_map/ppermute | solution.py:1032
  66.8 6.3 %collective-permute-start.12 = (bf16[128,192]{1,0:T(8,128)(2,1)S(1)}, bf16[128,192]{1,0:T(8,128)(2,1)S(1)}, u32[]{:S(2)}, u32[]{:S(2)}) collective-permute-start(bf16[128,192]{1,0:T(8,128)(2,1)S(1)} %get-tuple-element.91), channel_id=1, source_target_pairs={{0,24},{1,16},{2,8},{3,0},{4,28},{5,20},{6,12},{7,4},{8,25},{9,17}... | collective-permute-start | bytes 147464 | tf_op jit(solution)/shard_map/ppermute | solution.py:1035
  68.6 11.6 %collective-permute-start.13 = (bf16[128,192]{1,0:T(8,128)(2,1)S(1)}, bf16[128,192]{1,0:T(8,128)(2,1)S(1)}, u32[]{:S(2)}, u32[]{:S(2)}) collective-permute-start(bf16[128,192]{1,0:T(8,128)(2,1)S(1)} %get-tuple-element.92), channel_id=1, source_target_pairs={{0,16},{1,24},{2,0},{3,8},{4,20},{5,28},{6,4},{7,12},{8,17},{9,25}... | collective-permute-start | bytes 147464 | tf_op jit(solution)/shard_map/ppermute | solution.py:1035
  73.1 17.0 %collective-permute-start.14 = (bf16[128,192]{1,0:T(8,128)(2,1)S(1)}, bf16[128,192]{1,0:T(8,128)(2,1)S(1)}, u32[]{:S(2)}, u32[]{:S(2)}) collective-permute-start(bf16[128,192]{1,0:T(8,128)(2,1)S(1)} %get-tuple-element.93), channel_id=1, source_target_pairs={{0,8},{1,0},{2,24},{3,16},{4,12},{5,4},{6,28},{7,20},{8,9},{9,1},{... | collective-permute-start | bytes 147464 | tf_op jit(solution)/shard_map/ppermute | solution.py:1035
  76.7 13.4 %collective-permute-start.15 = (bf16[128,192]{1,0:T(8,128)(2,1)S(1)}, bf16[128,192]{1,0:T(8,128)(2,1)S(1)}, u32[]{:S(2)}, u32[]{:S(2)}) collective-permute-start(bf16[128,192]{1,0:T(8,128)(2,1)S(1)} %get-tuple-element.94), channel_id=1, source_target_pairs={{0,0},{1,8},{2,16},{3,24},{4,4},{5,12},{6,20},{7,28},{8,1},{9,9},{... | collective-permute-start | bytes 147464 | tf_op jit(solution)/shard_map/ppermute | solution.py:1035
  77.5 12.6 %copy-start.6 = (bf16[256,768]{1,0:T(8,128)(2,1)S(1)}, bf16[256,768]{1,0:T(8,128)(2,1)}, u32[]{:S(2)}) copy-start(bf16[256,768]{1,0:T(8,128)(2,1)} %copy-done.5) | copy-start | bytes 1179652
  77.5 12.6 %copy-start.7 = (bf16[192,768]{1,0:T(8,128)(2,1)S(1)}, bf16[192,768]{1,0:T(8,128)(2,1)}, u32[]{:S(2)}) copy-start(bf16[192,768]{1,0:T(8,128)(2,1)} %refs_6_.3) | copy-start | bytes 884740
  77.6 12.6 %copy-start.11 = (bf16[768,768]{1,0:T(8,128)(2,1)S(1)}, bf16[768,768]{1,0:T(8,128)(2,1)}, u32[]{:S(2)}) copy-start(bf16[768,768]{1,0:T(8,128)(2,1)} %refs_9_.3) | copy-start | bytes 3538948
  77.6 12.6 %copy-start.12 = (bf16[768,768]{1,0:T(8,128)(2,1)S(1)}, bf16[768,768]{1,0:T(8,128)(2,1)}, u32[]{:S(2)}) copy-start(bf16[768,768]{1,0:T(8,128)(2,1)} %refs_10_.3) | copy-start | bytes 3538948
  96.5 4.1 %collective-permute-start.22 = (bf16[912,768]{1,0:T(8,128)(2,1)S(1)}, bf16[912,768]{1,0:T(8,128)(2,1)S(1)}, u32[]{:S(2)}, u32[]{:S(2)}) collective-permute-start(bf16[912,768]{1,0:T(8,128)(2,1)S(1)} %get-tuple-element.105), channel_id=1, source_target_pairs={{0,4},{4,0},{8,12},{12,8},{16,20},{20,16},{24,28},{28,24},{1,5},{5... | collective-permute-start | bytes 4202504 | tf_op jit(solution)/shard_map/ppermute | solution.py:1020
  96.6 4.0 %collective-permute-start.23 = (bf16[4,112,576]{2,1,0:T(8,128)(2,1)S(1)}, bf16[4,112,576]{2,1,0:T(8,128)(2,1)S(1)}, u32[]{:S(2)}, u32[]{:S(2)}) collective-permute-start(bf16[4,112,576]{2,1,0:T(8,128)(2,1)S(1)} %get-tuple-element.106), channel_id=1, source_target_pairs={{0,4},{4,0},{8,12},{12,8},{16,20},{20,16},{24,28},{28,24},{1,5},{5... | collective-permute-start | bytes 1548296 | tf_op jit(solution)/shard_map/ppermute | solution.py:1020
  101.3 16.7 %collective-permute-start.24 = (bf16[112,576]{1,0:T(8,128)(2,1)S(1)}, bf16[112,576]{1,0:T(8,128)(2,1)S(1)}, u32[]{:S(2)}, u32[]{:S(2)}) collective-permute-start(bf16[112,576]{1,0:T(8,128)(2,1)S(1)} %get-tuple-element.107), channel_id=1, source_target_pairs={{0,3},{1,2},{2,1},{3,0},{4,7},{5,6},{6,5},{7,4},{8,11},{9,10},{10,... | collective-permute-start | bytes 387080 | tf_op jit(solution)/shard_map/ppermute | solution.py:1023
  114.4 16.1 %collective-permute-start.30 = (bf16[352,768]{1,0:T(8,128)(2,1)S(1)}, bf16[352,768]{1,0:T(8,128)(2,1)S(1)}, u32[]{:S(2)}, u32[]{:S(2)}) collective-permute-start(bf16[352,768]{1,0:T(8,128)(2,1)S(1)} %get-tuple-element.119), channel_id=1, source_target_pairs={{0,24},{4,28},{8,16},{12,20},{16,8},{20,12},{24,0},{28,4},{1,25},{... | collective-permute-start | bytes 1622024 | tf_op jit(solution)/shard_map/ppermute | solution.py:1020
  114.5 25.7 %collective-permute-start.31 = (bf16[352,768]{1,0:T(8,128)(2,1)S(1)}, bf16[352,768]{1,0:T(8,128)(2,1)S(1)}, u32[]{:S(2)}, u32[]{:S(2)}) collective-permute-start(bf16[352,768]{1,0:T(8,128)(2,1)S(1)} %get-tuple-element.120), channel_id=1, source_target_pairs={{0,16},{4,20},{8,24},{12,28},{16,0},{20,4},{24,8},{28,12},{1,17},{... | collective-permute-start | bytes 1622024 | tf_op jit(solution)/shard_map/ppermute | solution.py:1020
  114.6 25.6 %collective-permute-start.32 = (bf16[352,768]{1,0:T(8,128)(2,1)S(1)}, bf16[352,768]{1,0:T(8,128)(2,1)S(1)}, u32[]{:S(2)}, u32[]{:S(2)}) collective-permute-start(bf16[352,768]{1,0:T(8,128)(2,1)S(1)} %get-tuple-element.121), channel_id=1, source_target_pairs={{0,8},{4,12},{8,0},{12,4},{16,24},{20,28},{24,16},{28,20},{1,9},{5... | collective-permute-start | bytes 1622024 | tf_op jit(solution)/shard_map/ppermute | solution.py:1020
  118.0 6.4 %collective-permute-start.25 = (bf16[112,576]{1,0:T(8,128)(2,1)S(1)}, bf16[112,576]{1,0:T(8,128)(2,1)S(1)}, u32[]{:S(2)}, u32[]{:S(2)}) collective-permute-start(bf16[112,576]{1,0:T(8,128)(2,1)S(1)} %get-tuple-element.108), channel_id=1, source_target_pairs={{0,2},{1,3},{2,0},{3,1},{4,6},{5,7},{6,4},{7,5},{8,10},{9,11},{10,... | collective-permute-start | bytes 387080 | tf_op jit(solution)/shard_map/ppermute | solution.py:1023
  118.0 8.0 %collective-permute-start.26 = (bf16[112,576]{1,0:T(8,128)(2,1)S(1)}, bf16[112,576]{1,0:T(8,128)(2,1)S(1)}, u32[]{:S(2)}, u32[]{:S(2)}) collective-permute-start(bf16[112,576]{1,0:T(8,128)(2,1)S(1)} %get-tuple-element.109), channel_id=1, source_target_pairs={{0,1},{1,0},{2,3},{3,2},{4,5},{5,4},{6,7},{7,6},{8,9},{9,8},{10,11... | collective-permute-start | bytes 387080 | tf_op jit(solution)/shard_map/ppermute | solution.py:1023
  126.6 18.0 %collective-permute-start.27 = (bf16[256,768]{1,0:T(8,128)(2,1)S(1)}, bf16[256,768]{1,0:T(8,128)(2,1)S(1)}, u32[]{:S(2)}, u32[]{:S(2)}) collective-permute-start(bf16[256,768]{1,0:T(8,128)(2,1)S(1)} %get-tuple-element.111), channel_id=1, source_target_pairs={{0,3},{1,0},{2,1},{3,2},{4,7},{5,4},{6,5},{7,6},{8,11},{9,8},{10,9... | collective-permute-start | bytes 1179656 | tf_op jit(solution)/shard_map/ppermute | solution.py:1026
  141.1 30.0 %collective-permute-start.35 = (bf16[320,768]{1,0:T(8,128)(2,1)S(1)}, bf16[320,768]{1,0:T(8,128)(2,1)S(1)}, u32[]{:S(2)}, u32[]{:S(2)}) collective-permute-start(bf16[320,768]{1,0:T(8,128)(2,1)S(1)} %plane_share.1.refs_7_), channel_id=1, source_target_pairs={{0,8},{4,12},{8,0},{12,4},{16,24},{20,28},{24,16},{28,20},{1,9},{5... | collective-permute-start | bytes 1474568 | tf_op jit(solution)/shard_map/ppermute | solution.py:1020
  141.4 29.7 %collective-permute-start.34 = (bf16[320,768]{1,0:T(8,128)(2,1)S(1)}, bf16[320,768]{1,0:T(8,128)(2,1)S(1)}, u32[]{:S(2)}, u32[]{:S(2)}) collective-permute-start(bf16[320,768]{1,0:T(8,128)(2,1)S(1)} %plane_share.1.refs_7_), channel_id=1, source_target_pairs={{0,16},{4,20},{8,24},{12,28},{16,0},{20,4},{24,8},{28,12},{1,17},{... | collective-permute-start | bytes 1474568 | tf_op jit(solution)/shard_map/ppermute | solution.py:1020
  142.8 28.3 %collective-permute-start.33 = (bf16[320,768]{1,0:T(8,128)(2,1)S(1)}, bf16[320,768]{1,0:T(8,128)(2,1)S(1)}, u32[]{:S(2)}, u32[]{:S(2)}) collective-permute-start(bf16[320,768]{1,0:T(8,128)(2,1)S(1)} %plane_share.1.refs_7_), channel_id=1, source_target_pairs={{0,24},{4,28},{8,16},{12,20},{16,8},{20,12},{24,0},{28,4},{1,25},{... | collective-permute-start | bytes 1474568 | tf_op jit(solution)/shard_map/ppermute | solution.py:1020
  144.6 26.4 %collective-permute-start.28 = (bf16[256,768]{1,0:T(8,128)(2,1)S(1)}, bf16[256,768]{1,0:T(8,128)(2,1)S(1)}, u32[]{:S(2)}, u32[]{:S(2)}) collective-permute-start(bf16[256,768]{1,0:T(8,128)(2,1)S(1)} %get-tuple-element.112), channel_id=1, source_target_pairs={{0,2},{1,3},{2,0},{3,1},{4,6},{5,7},{6,4},{7,5},{8,10},{9,11},{10,... | collective-permute-start | bytes 1179656 | tf_op jit(solution)/shard_map/ppermute | solution.py:1026
  144.6 26.4 %collective-permute-start.29 = (bf16[256,768]{1,0:T(8,128)(2,1)S(1)}, bf16[256,768]{1,0:T(8,128)(2,1)S(1)}, u32[]{:S(2)}, u32[]{:S(2)}) collective-permute-start(bf16[256,768]{1,0:T(8,128)(2,1)S(1)} %get-tuple-element.113), channel_id=1, source_target_pairs={{0,1},{1,2},{2,3},{3,0},{4,5},{5,6},{6,7},{7,4},{8,9},{9,10},{10,1... | collective-permute-start | bytes 1179656 | tf_op jit(solution)/shard_map/ppermute | solution.py:1026
  171.7 4.0 %collective-permute-start.36 = (bf16[1280,768]{1,0:T(8,128)(2,1)S(1)}, bf16[1280,768]{1,0:T(8,128)(2,1)S(1)}, u32[]{:S(2)}, u32[]{:S(2)}) collective-permute-start(bf16[1280,768]{1,0:T(8,128)(2,1)S(1)} %stack.13.refs_1_.refs_2_), channel_id=1, source_target_pairs={{0,4},{4,0},{8,12},{12,8},{16,20},{20,16},{24,28},{28,24},{1,5},{5... | collective-permute-start | bytes 5898248 | tf_op jit(solution)/shard_map/ppermute | solution.py:1020
  171.8 4.0 %copy-start.10 = (s32[2]{0:T(128)S(1)}, s32[2]{0:T(128)}, u32[]{:S(2)}) copy-start(s32[2]{0:T(128)} %pad_add_fusion.refs_0_) | copy-start | bytes 28
  (5 other events, 5.2 us)
where the time goes:
time: 183 us
  waiting for transfers between devices  85 us (46%)
  starting transfers between devices  57.9 us (32%)
  Pallas kernels  33 us (18%)
  local copies, waits for them, and re-layouts  3.83 us (2%)
    pallas_call x14, Pallas kernels, local_call(): pl.pallas_call(body, out_shape=[jax.ShapeDtypeStruct(s, d) for s, d in ou...  33 us
    ppermute x3, waiting for transfers between devices, around_z(): return lax.ppermute(value, 'fsdp', [(i, (i + k) % n_z) for i in range(n_z)])  24.7 us
    ppermute x6, starting transfers between devices, over_z(): return lax.ppermute(value, 'fsdp', [(i, i ^ k) for i in range(n_z)])  21.7 us
    ppermute x16, waiting for transfers between devices, over_ctx(): return lax.ppermute(value, 'ctx', [(i, i ^ k) for i in range(n_ctx)])  19.7 us
    ppermute x6, waiting for transfers between devices, along_z(): return lax.ppermute(value, 'fsdp', pairs)  15.7 us
    ppermute x6, waiting for transfers between devices, over_z(): return lax.ppermute(value, 'fsdp', [(i, i ^ k) for i in range(n_z)])  13.1 us
    ppermute x16, starting transfers between devices, over_ctx(): return lax.ppermute(value, 'ctx', [(i, i ^ k) for i in range(n_ctx)])  13.1 us
    ppermute x6, waiting for transfers between devices, over_both(): lax.ppermute(value, ('ctx', 'fsdp'), [(a * n_z + b, d * n_z + e) for a, b...  11.8 us
  transfers between devices with their start and end apart: 37, of which 16 were waited for; matrix products, arithmetic and copies ran while one was open for 0% of the time, Pallas kernels for 9%

commit v1 on v0

--- a/solution.py
+++ b/solution.py
@@ -845,12 +845,12 @@
 
 
 def ffn_body(places, *refs):
-    line = refs[0:7]
-    up_w, down_w, up_b, vec, out_w = refs[7:12]
-    atts = refs[12:16]
-    outs = refs[16:20]
-    sums, si, gb, active, hidden_grad, att = refs[20:26]
-    second, norms = refs[26:]
+    line = refs[0:6]
+    up_w, down_w, up_b, vec, out_w = refs[6:11]
+    atts = refs[11:15]
+    outs = refs[15:19]
+    sums, si, gb, active, hidden_grad, att = refs[19:25]
+    second, norms = refs[25:]
     c, z = places[0], places[1]
     rows = line[0].shape[0] // 2
     width = up_w.shape[0]
@@ -858,7 +858,14 @@
     gain, shift = vec[2:3, :], vec[3:4, :]
     for k in range(GROUPS):
         at = slice(k * rows, (k + 1) * rows)
-        piece = line[0] if k == 0 else line[k][...] + line[7 - k][...]
+        if k == 0:
+            piece = line[0]
+        elif k == 2:
+            piece = line[2][...] + line[5][...]
+        else:
+            ends = line[3][...]
+            here = z == (0 if k == 1 else GROUPS - 1)
+            piece = line[1 if k == 1 else 4][...] + jnp.where(here, ends, jnp.zeros_like(ends))
         norm, _ = normed(piece[0:rows, :].astype(F32))
         norms[at, :] = norm
         si[at, :] = (norm * gain + shift).astype(BF16)
@@ -920,7 +927,7 @@
 
 
 def spread_body(places, near, far, *refs):
-    up_dw, down_dw, out_dw, qkv_dw, vec, up_db, bias, buf, box, qkv_box = refs
+    up_dw, down_dw, out_dw, qkv_dw, v0, v1, v2, v3, v4, up_db, bias, buf, box, qkv_box = refs
     c = places[0]
     core, group = c % 2, c // 2
     shard = out_dw.shape[0]
@@ -957,13 +964,12 @@
                 g, :, slot * GROUP_COLS : (slot + 1) * GROUP_COLS
             ]
     total = box[0] + box[1] + box[2] + box[3]
-    bias[...] = total[0:1, :]
-    for slot in range(3):
-        vec[slot : slot + 1, :] = total[1:2, slot * shard : (slot + 1) * shard]
-    vec[3:4, :] = total[2:3, 0:shard]
-    vec[4:5, :] = total[2:3, shard : 2 * shard]
-    up_db[0:1, 0:shard] = total[2:3, 2 * shard :]
-    up_db[0:1, shard:] = total[3:4, :]
+    bias[...] = total[0:1, :].reshape(three)
+    for slot, vec in enumerate((v0, v1, v2)):
+        vec[...] = total[1:2, slot * shard : (slot + 1) * shard].reshape(shard)
+    v3[...] = total[2:3, 0:shard].reshape(shard)
+    v4[...] = total[2:3, shard : 2 * shard].reshape(shard)
+    up_db[...] = jnp.concatenate([total[2:3, 2 * shard :], total[3:4, :]], axis=1).reshape(4 * shard)
 
 
 def token_body(places, xg, vec, ca, ffn, *refs):
@@ -1070,10 +1076,11 @@
         through=[xg_line],
     )
     up, down = [xg_line], [xg_line]
-    for i in range(n_z - 1):
+    for i in range(n_z - 2):
         up.append(along_z(up[-1], 1, i))
         down.append(along_z(down[-1], -1, i))
-    line = up + down[1:]
+    ends = lax.ppermute(up[-1] + down[-1], "fsdp", [(n_z - 2, n_z - 1), (1, 0)])
+    line = up + [ends] + down[1:]
     cos_tab, sin_tab = rotary_tables(rows, n_ctx)
     fi, w, q, kv, cos, sin = local_call(
         "qkv",
@@ -1111,6 +1118,7 @@
             pltpu.VMEM((GROUPS, rows, GROUP_COLS), BF16),
         ],
         flops=2 * 7 * 256 * GROUP_HEADS * near_rows * 2 * near_rows,
+        after=[up[1], down[1]],
     )
     att = [
         over_both(
@@ -1138,6 +1146,7 @@
             pltpu.VMEM((GROUPS, EXTRA, three), F32),
         ],
         flops=2 * 2 * near_rows * width * three,
+        after=[up[2], down[2]],
     )
     ca_sends = sends
     chunk = -(-(width + hid + shard) // (n_ctx * EXTRA)) * EXTRA
@@ -1205,7 +1214,7 @@
         [((GROUPS * (chunk + part), width), BF16)],
         after=from_line,
     )
-    up_dw, down_dw, out_dw, qkv_dw, sums, up_db, qkv_db = local_call(
+    up_dw, down_dw, out_dw, qkv_dw, *sums, up_db, qkv_db = local_call(
         "spread",
         spread_body,
         places,
@@ -1215,9 +1224,9 @@
             ((hid, width), F32),
             ((shard, width), F32),
             ((shard, 3 * width), F32),
-            ((8, shard), F32),
-            ((1, hid), F32),
-            ((1, three), F32),
+            *[((shard,), F32)] * 5,
+            ((hid,), F32),
+            ((three,), F32),
         ],
         [
             pltpu.VMEM((n_ctx * chunk, width), F32),
@@ -1243,11 +1252,11 @@
         sums[3],
         sums[4],
         qkv_dw,
-        qkv_db[0],
+        qkv_db,
         out_dw,
         sums[2],
         up_dw,
-        up_db[0],
+        up_db,
         down_dw,
         sums[2],
     )

time: 183 us -> 176 us (0.962)
  starting transfers between devices: 57.9 us -> 52.5 us
    ppermute x6, starting transfers between devices: 21.7 us -> 14.6 us  [over_z(): return lax.ppermute(value, 'fsdp', [(i, i ^ k) for i in range(n_z)])]
    ppermute x6 -> x4, waiting for transfers between devices: 15.7 us -> 12.2 us  [along_z(): return lax.ppermute(value, 'fsdp', pairs)]
    ppermute x6, starting transfers between devices: 10.1 us -> 12.6 us  [over_both(): lax.ppermute(value, ('ctx', 'fsdp'), [(a * n_z + b, d * n_z + e) for a, b...]
    ppermute x6, waiting for transfers between devices: 11.8 us -> 14.3 us  [over_both(): lax.ppermute(value, ('ctx', 'fsdp'), [(a * n_z + b, d * n_z + e) for a, b...]
    ppermute x6 -> x4, starting transfers between devices: 8.72 us -> 7.83 us  [along_z(): return lax.ppermute(value, 'fsdp', pairs)]
  transfers between devices with their start and end apart: 37 -> 36, of which waited for: 16 -> 16; matrix products, arithmetic and copies ran while one was open for 0% -> 0% of each run, Pallas kernels for 9% -> 10%
where the time goes in v1:
time: 176 us
  waiting for transfers between devices  85.1 us (48%)
  starting transfers between devices  52.5 us (30%)
  Pallas kernels  33.4 us (19%)
  local copies, waits for them, and re-layouts  2.94 us (2%)
    pallas_call x14, Pallas kernels, local_call(): pl.pallas_call(body, out_shape=[jax.ShapeDtypeStruct(s, d) for s, d in ou...  33.4 us
    ppermute x3, waiting for transfers between devices, around_z(): return lax.ppermute(value, 'fsdp', [(i, (i + k) % n_z) for i in range(n_z)])  24.1 us
    ppermute x16, waiting for transfers between devices, over_ctx(): return lax.ppermute(value, 'ctx', [(i, i ^ k) for i in range(n_ctx)])  21.3 us
    ppermute x6, starting transfers between devices, over_z(): return lax.ppermute(value, 'fsdp', [(i, i ^ k) for i in range(n_z)])  14.6 us
    ppermute x6, waiting for transfers between devices, over_both(): lax.ppermute(value, ('ctx', 'fsdp'), [(a * n_z + b, d * n_z + e) for a, b...  14.3 us
    ppermute x6, waiting for transfers between devices, over_z(): return lax.ppermute(value, 'fsdp', [(i, i ^ k) for i in range(n_z)])  13.3 us
    ppermute x16, starting transfers between devices, over_ctx(): return lax.ppermute(value, 'ctx', [(i, i ^ k) for i in range(n_ctx)])  13.2 us
    ppermute x6, starting transfers between devices, over_both(): lax.ppermute(value, ('ctx', 'fsdp'), [(a * n_z + b, d * n_z + e) for a, b...  12.6 us
  transfers between devices with their start and end apart: 36, of which 16 were waited for; matrix products, arithmetic and copies ran while one was open for 0% of the time, Pallas kernels for 10%

profile of v1, /device:TPU:0, one launch (start us, length us, event | category | flops | bytes accessed | tf_op | source)
XLA Modules:
  0.0 175.6 jit_solution(8407588067738072387)
XLA Ops:
  1.2 3.3 %pack.1 = (bf16[112,576]{1,0:T(8,128)(2,1)}, bf16[256,768]{1,0:T(8,128)(2,1)}, bf16[256,768]{1,0:T(8,128)(2,1)}, bf16[96,768]{1,0:T(8,128)(2,1)}) custom-call(s32[2]{0:T(128)} %pad_add_fusion.refs_0_, bf16[192,768]{1,0:T(8,128)(2,1)} %refs_6_.3, bf16[128,768]{1,0:T(8,128)(2,1)} %bitcast.6, bf16[128,768]{1,0:T(8,128)(2,1)} %bitcast.8, ...), custom_call_target="tpu_custom_call" | custom-call | bytes 1066368 | tf_op jit(solution)/shard_map/pack/pallas_call | solution.py:452
  4.5 4.0 %collective-permute-start.2 = (bf16[256,768]{1,0:T(8,128)(2,1)}, bf16[256,768]{1,0:T(8,128)(2,1)S(1)}, u32[]{:S(2)}, u32[]{:S(2)}) collective-permute-start(bf16[256,768]{1,0:T(8,128)(2,1)} %get-tuple-element.78.refs_10_.refs_8_.refs_7_.refs_11_), channel_id=1, source_target_pairs={{0,24},{4,28},{8,16},{12,20},{16,8},{20,12},{24,0},{28,4},{1,25},{... | collective-permute-start | bytes 1179656 | tf_op jit(solution)/shard_map/ppermute | solution.py:1026
  9.1 2.0 %collective-permute-start.5 = (bf16[112,576]{1,0:T(8,128)(2,1)}, bf16[112,576]{1,0:T(8,128)(2,1)S(1)}, u32[]{:S(2)}, u32[]{:S(2)}) collective-permute-start(bf16[112,576]{1,0:T(8,128)(2,1)} %get-tuple-element.80.refs_8_), channel_id=1, source_target_pairs={{0,1},{1,0},{2,3},{3,2},{4,5},{5,4},{6,7},{7,6},{8,9},{9,8},{10,11... | collective-permute-start | bytes 387080 | tf_op jit(solution)/shard_map/ppermute | solution.py:1029
  11.1 2.6 %collective-permute-start.4 = (bf16[112,576]{1,0:T(8,128)(2,1)}, bf16[112,576]{1,0:T(8,128)(2,1)S(1)}, u32[]{:S(2)}, u32[]{:S(2)}) collective-permute-start(bf16[112,576]{1,0:T(8,128)(2,1)} %get-tuple-element.80.refs_8_), channel_id=1, source_target_pairs={{0,2},{1,3},{2,0},{3,1},{4,6},{5,7},{6,4},{7,5},{8,10},{9,11},{10,... | collective-permute-start | bytes 387080 | tf_op jit(solution)/shard_map/ppermute | solution.py:1029
  13.7 2.4 %collective-permute-done.5.refs_7_ = bf16[112,576]{1,0:T(8,128)(2,1)S(1)} collective-permute-done((bf16[112,576]{1,0:T(8,128)(2,1)}, bf16[112,576]{1,0:T(8,128)(2,1)S(1)}, u32[]{:S(2)}, u32[]{:S(2)}) %collective-permute-start.5) | collective-permute-done | bytes 129056 | tf_op jit(solution)/shard_map/ppermute | solution.py:1029
  16.1 4.1 %collective-permute-start.3 = (bf16[112,576]{1,0:T(8,128)(2,1)}, bf16[112,576]{1,0:T(8,128)(2,1)S(1)}, u32[]{:S(2)}, u32[]{:S(2)}) collective-permute-start(bf16[112,576]{1,0:T(8,128)(2,1)} %get-tuple-element.80.refs_8_), channel_id=1, source_target_pairs={{0,3},{1,2},{2,1},{3,0},{4,7},{5,6},{6,5},{7,4},{8,11},{9,10},{10,... | collective-permute-start | bytes 387080 | tf_op jit(solution)/shard_map/ppermute | solution.py:1029
  20.2 1.8 %collective-permute-done.4.refs_6_ = bf16[112,576]{1,0:T(8,128)(2,1)S(1)} collective-permute-done((bf16[112,576]{1,0:T(8,128)(2,1)}, bf16[112,576]{1,0:T(8,128)(2,1)S(1)}, u32[]{:S(2)}, u32[]{:S(2)}) %collective-permute-start.4) | collective-permute-done | bytes 129056 | tf_op jit(solution)/shard_map/ppermute | solution.py:1029
  22.0 1.6 collective-permute-done.3.refs_5_
  23.6 2.6 %collective-permute-done.1.refs_2_.refs_8_.refs_6_.refs_5_ = bf16[256,768]{1,0:T(8,128)(2,1)S(1)} collective-permute-done((bf16[256,768]{1,0:T(8,128)(2,1)}, bf16[256,768]{1,0:T(8,128)(2,1)S(1)}, u32[]{:S(2)}, u32[]{:S(2)}) %collective-permute-start.1) | collective-permute-done | bytes 393248 | tf_op jit(solution)/shard_map/ppermute | solution.py:1026
  26.5 0.9 copy-done.5
  28.0 0.8 collect.1
  29.6 1.3 collective-permute-start.8
  30.9 4.6 %collective-permute-start.6 = (bf16[256,768]{1,0:T(8,128)(2,1)}, bf16[256,768]{1,0:T(8,128)(2,1)S(1)}, u32[]{:S(2)}, u32[]{:S(2)}) collective-permute-start(bf16[256,768]{1,0:T(8,128)(2,1)} %get-tuple-element.81.refs_16_), channel_id=1, source_target_pairs={{0,1},{1,2},{2,3},{4,5},{5,6},{6,7},{8,9},{9,10},{10,11},{12,13},{... | collective-permute-start | bytes 1179656 | tf_op jit(solution)/shard_map/ppermute | solution.py:1038
  35.5 2.0 %qkv.1 = (bf16[512,768]{1,0:T(8,128)(2,1)S(1)}, bf16[768,576]{1,0:T(8,128)(2,1)S(1)}, bf16[512,192]{1,0:T(8,128)(2,1)S(1)}, bf16[1024,192]{1,0:T(8,128)(2,1)S(1)...) custom-call(s32[2]{0:T(128)S(1)} %copy-done.6, f32[1024,128]{1,0:T(8,128)S(1)} %copy-done.3, f32[1024,128]{1,0:T(8,128)S(1)} %copy-done.2, ...), custom_call_target="tpu_custom_call" | custom-call | flops 603979776 | bytes 6334464 | tf_op jit(solution)/shard_map/qkv/pallas_call | solution.py:452
  38.9 4.3 %collective-permute-done.8.refs_2_.refs_12_ = bf16[256,768]{1,0:T(8,128)(2,1)S(1)} collective-permute-done((bf16[256,768]{1,0:T(8,128)(2,1)}, bf16[256,768]{1,0:T(8,128)(2,1)S(1)}, u32[]{:S(2)}, u32[]{:S(2)}) %collective-permute-start.8) | collective-permute-done | bytes 393248 | tf_op jit(solution)/shard_map/ppermute | solution.py:1038
  43.2 1.3 collective-permute-start.9
  45.2 8.0 %attend.1 = (bf16[128,192]{1,0:T(8,128)(2,1)S(1)}, bf16[128,192]{1,0:T(8,128)(2,1)S(1)}, bf16[128,192]{1,0:T(8,128)(2,1)S(1)}, bf16[128,192]{1,0:T(8,128)(2,1)S(...) custom-call(s32[2]{0:T(128)S(1)} %copy-done.6, ...), custom_call_target="tpu_custom_call" | custom-call | flops 5637144576 | bytes 4620288 | tf_op jit(solution)/shard_map/attend/pallas_call | solution.py:452
  53.3 7.9 %collective-permute-done.9.refs_2_.refs_11_ = bf16[256,768]{1,0:T(8,128)(2,1)S(1)} collective-permute-done((bf16[256,768]{1,0:T(8,128)(2,1)S(1)}, bf16[256,768]{1,0:T(8,128)(2,1)S(1)}, u32[]{:S(2)}, u32[]{:S(2)}) %collective-permute-start.9) | collective-permute-done | bytes 393248 | tf_op jit(solution)/shard_map/ppermute | solution.py:1038
  61.2 1.3 collective-permute-start.20
  62.6 2.9 %collective-permute-start.16 = (bf16[128,192]{1,0:T(8,128)(2,1)S(1)}, bf16[128,192]{1,0:T(8,128)(2,1)S(1)}, u32[]{:S(2)}, u32[]{:S(2)}) collective-permute-start(bf16[128,192]{1,0:T(8,128)(2,1)S(1)} %get-tuple-element.96), channel_id=1, source_target_pairs={{0,24},{1,16},{2,8},{3,0},{4,28},{5,20},{6,12},{7,4},{8,25},{9,17}... | collective-permute-start | bytes 147464 | tf_op jit(solution)/shard_map/ppermute | solution.py:1041
  65.5 5.8 %collective-permute-start.17 = (bf16[128,192]{1,0:T(8,128)(2,1)S(1)}, bf16[128,192]{1,0:T(8,128)(2,1)S(1)}, u32[]{:S(2)}, u32[]{:S(2)}) collective-permute-start(bf16[128,192]{1,0:T(8,128)(2,1)S(1)} %get-tuple-element.97), channel_id=1, source_target_pairs={{0,16},{1,24},{2,0},{3,8},{4,20},{5,28},{6,4},{7,12},{8,17},{9,25}... | collective-permute-start | bytes 147464 | tf_op jit(solution)/shard_map/ppermute | solution.py:1041
  71.2 1.7 collective-permute-start.18
  73.0 0.8 collective-permute-start.19
  73.9 2.6 %joined.1 = (f32[128,768]{1,0:T(8,128)S(1)}, bf16[128,768]{1,0:T(8,128)(2,1)S(1)}, bf16[128,768]{1,0:T(8,128)(2,1)S(1)}, bf16[128,768]{1,0:T(8,128)(2,1)S(1)}, f...) custom-call(s32[2]{0:T(128)S(1)} %copy-done.6, bf16[256,768]{1,0:T(8,128)(2,1)S(1)} %collective-permute-done.7.refs_1_.refs_14_, ...), custom_call_target="tpu_custom_call" | custom-call | flops 905969664 | bytes 8093696 | tf_op jit(solution)/shard_map/joined/pallas_call | solution.py:452
  76.5 14.3 %collective-permute-done.18.refs_4_ = bf16[128,192]{1,0:T(8,128)(2,1)S(1)} collective-permute-done((bf16[128,192]{1,0:T(8,128)(2,1)S(1)}, bf16[128,192]{1,0:T(8,128)(2,1)S(1)}, u32[]{:S(2)}, u32[]{:S(2)}) %collective-permute-start.18) | collective-permute-done | bytes 49184 | tf_op jit(solution)/shard_map/ppermute | solution.py:1041
  90.8 4.3 %ffn.1 = (f32[256,768]{1,0:T(8,128)S(1)}, bf16[256,768]{1,0:T(8,128)(2,1)S(1)}, bf16[256,768]{1,0:T(8,128)(2,1)S(1)}, bf16[256,768]{1,0:T(8,128)(2,1)S(1)}, bf16...) custom-call(s32[2]{0:T(128)S(1)} %copy-done.6, ...), custom_call_target="tpu_custom_call" | custom-call | flops 2415919104 | bytes 10569216 | tf_op jit(solution)/shard_map/ffn/pallas_call | solution.py:452
  95.2 2.5 %ffn_dw.1 = (f32[896,768]{1,0:T(8,128)S(1)}, bf16[912,768]{1,0:T(8,128)(2,1)S(1)}) custom-call(s32[2]{0:T(128)S(1)} %copy-done.6, bf16[16,768]{1,0:T(8,128)(2,1)S(1)} %get-tuple-element.103.refs_1_.refs_2_, bf16[512,192]{1,0:T(8,128)(2,1)S(1)} %get-tuple-element.104.refs_2_, bf16[512,768]{1,0:T(8,128)(2,1)S(1)} %get-tuple-element.105.refs_3_, ...), custom_call_target="tpu_custom_call" | custom-call | flops 1207959552 | bytes 7520256 | tf_op jit(solution)/shard_map/ffn_dw/pallas_call | solution.py:452
  98.2 3.5 %collective-permute-done.22.refs_3_ = bf16[4,112,576]{2,1,0:T(8,128)(2,1)S(1)} collective-permute-done((bf16[4,112,576]{2,1,0:T(8,128)(2,1)S(1)}, bf16[4,112,576]{2,1,0:T(8,128)(2,1)S(1)}, u32[]{:S(2)}, u32[]{:S(2)}) %collective-permute-start.22) | collective-permute-done | bytes 516128 | tf_op jit(solution)/shard_map/ppermute | solution.py:1026
  101.7 0.7 qkv_pair.1
  102.4 5.4 %collective-permute-start.23 = (bf16[112,576]{1,0:T(8,128)(2,1)S(1)}, bf16[112,576]{1,0:T(8,128)(2,1)S(1)}, u32[]{:S(2)}, u32[]{:S(2)}) collective-permute-start(bf16[112,576]{1,0:T(8,128)(2,1)S(1)} %get-tuple-element.111), channel_id=1, source_target_pairs={{0,3},{1,2},{2,1},{3,0},{4,7},{5,6},{6,5},{7,4},{8,11},{9,10},{10,... | collective-permute-start | bytes 387080 | tf_op jit(solution)/shard_map/ppermute | solution.py:1029
  107.8 0.9 ffn_pair.1
  108.6 1.5 collective-permute-start.29
  110.1 0.8 collective-permute-start.30
  110.9 1.4 collective-permute-start.31
  112.8 6.1 %collective-permute-done.24.refs_5_ = bf16[112,576]{1,0:T(8,128)(2,1)S(1)} collective-permute-done((bf16[112,576]{1,0:T(8,128)(2,1)S(1)}, bf16[112,576]{1,0:T(8,128)(2,1)S(1)}, u32[]{:S(2)}, u32[]{:S(2)}) %collective-permute-start.24) | collective-permute-done | bytes 129056 | tf_op jit(solution)/shard_map/ppermute | solution.py:1029
  118.9 1.4 collective-permute-done.25.refs_6_
  121.0 2.2 %collective-permute-start.26 = (bf16[256,768]{1,0:T(8,128)(2,1)S(1)}, bf16[256,768]{1,0:T(8,128)(2,1)S(1)}, u32[]{:S(2)}, u32[]{:S(2)}) collective-permute-start(bf16[256,768]{1,0:T(8,128)(2,1)S(1)} %get-tuple-element.115), channel_id=1, source_target_pairs={{0,3},{1,0},{2,1},{3,2},{4,7},{5,4},{6,5},{7,6},{8,11},{9,8},{10,9... | collective-permute-start | bytes 1179656 | tf_op jit(solution)/shard_map/ppermute | solution.py:1032
  123.1 1.7 collective-permute-done.29.refs_2_.refs_5_
  124.8 10.4 %collective-permute-done.30.refs_3_.refs_6_ = bf16[352,768]{1,0:T(8,128)(2,1)S(1)} collective-permute-done((bf16[352,768]{1,0:T(8,128)(2,1)S(1)}, bf16[352,768]{1,0:T(8,128)(2,1)S(1)}, u32[]{:S(2)}, u32[]{:S(2)}) %collective-permute-start.30) | collective-permute-done | bytes 540704 | tf_op jit(solution)/shard_map/ppermute | solution.py:1026
  135.9 0.8 plane_share.1.refs_7_
  137.0 1.0 collective-permute-start.33
  138.1 2.2 %collective-permute-start.32 = (bf16[320,768]{1,0:T(8,128)(2,1)S(1)}, bf16[320,768]{1,0:T(8,128)(2,1)S(1)}, u32[]{:S(2)}, u32[]{:S(2)}) collective-permute-start(bf16[320,768]{1,0:T(8,128)(2,1)S(1)} %plane_share.1.refs_7_), channel_id=1, source_target_pairs={{0,24},{4,28},{8,16},{12,20},{16,8},{20,12},{24,0},{28,4},{1,25},{... | collective-permute-start | bytes 1474568 | tf_op jit(solution)/shard_map/ppermute | solution.py:1026
  140.3 0.9 collective-permute-start.28
  141.1 24.1 %collective-permute-done.27.refs_2_.refs_3_ = bf16[256,768]{1,0:T(8,128)(2,1)S(1)} collective-permute-done((bf16[256,768]{1,0:T(8,128)(2,1)S(1)}, bf16[256,768]{1,0:T(8,128)(2,1)S(1)}, u32[]{:S(2)}, u32[]{:S(2)}) %collective-permute-start.27) | collective-permute-done | bytes 393248 | tf_op jit(solution)/shard_map/ppermute | solution.py:1032
  166.0 1.8 %token_.1 = (bf16[128,768]{1,0:T(8,128)(2,1)}, f32[128,768]{1,0:T(8,128)}) custom-call(s32[2]{0:T(128)S(1)} %copy-done.6, bf16[1280,768]{1,0:T(8,128)(2,1)S(1)} %stack.13.refs_1_.refs_2_, bf16[256,768]{1,0:T(8,128)(2,1)S(1)} %collective-permute-done.28.refs_3_.refs_2_, bf16[256,768]{1,0:T(8,128)(2,1)S(1)} %collective-permute-done.27.refs_2_.refs_3_, ...), custom_call_target="tpu_custom_call" | custom-call | bytes 4988928 | tf_op jit(solution)/shard_map/token/pallas_call | solution.py:452
  167.8 2.1 %collective-permute-done.35.refs_1_ = bf16[1280,768]{1,0:T(8,128)(2,1)S(1)} collective-permute-done((bf16[1280,768]{1,0:T(8,128)(2,1)S(1)}, bf16[1280,768]{1,0:T(8,128)(2,1)S(1)}, u32[]{:S(2)}, u32[]{:S(2)}) %collective-permute-start.35) | collective-permute-done | bytes 1966112 | tf_op jit(solution)/shard_map/ppermute | solution.py:1026
  170.0 4.4 %spread.1 = (f32[768,768]{1,0:T(8,128)}, f32[768,768]{1,0:T(8,128)}, f32[192,768]{1,0:T(8,128)}, f32[192,2304]{1,0:T(8,128)}, f32[192]{0:T(256)}, /*index=5*/f32...) custom-call(s32[2]{0:T(128)S(1)} %copy-done.7, ...), custom_call_target="tpu_custom_call" | custom-call | bytes 11019264 | tf_op jit(solution)/shard_map/spread/pallas_call | solution.py:452
  174.4 1.2 copy.39
  (66 shorter events, 8.7 us)
Async XLA Ops:
  1.2 34.3 %copy-start.2 = (f32[1024,128]{1,0:T(8,128)S(1)}, f32[1024,128]{1,0:T(8,128)}, u32[]{:S(2)}) copy-start(f32[1024,128]{1,0:T(8,128)} %constant.14.clone.refs_2_) | copy-start | bytes 1572868
  1.2 34.3 %copy-start.3 = (f32[1024,128]{1,0:T(8,128)S(1)}, f32[1024,128]{1,0:T(8,128)}, u32[]{:S(2)}) copy-start(f32[1024,128]{1,0:T(8,128)} %constant.13.clone.refs_1_) | copy-start | bytes 1572868
  4.5 31.0 %copy-start = (bf16[256,768]{1,0:T(8,128)(2,1)S(1)}, bf16[256,768]{1,0:T(8,128)(2,1)}, u32[]{:S(2)}) copy-start(bf16[256,768]{1,0:T(8,128)(2,1)} %get-tuple-element.78.refs_10_.refs_8_.refs_7_.refs_11_) | copy-start | bytes 1179652
  4.5 19.1 %collective-permute-start.2 = (bf16[256,768]{1,0:T(8,128)(2,1)}, bf16[256,768]{1,0:T(8,128)(2,1)S(1)}, u32[]{:S(2)}, u32[]{:S(2)}) collective-permute-start(bf16[256,768]{1,0:T(8,128)(2,1)} %get-tuple-element.78.refs_10_.refs_8_.refs_7_.refs_11_), channel_id=1, source_target_pairs={{0,24},{4,28},{8,16},{12,20},{16,8},{20,12},{24,0},{28,4},{1,25},{... | collective-permute-start | bytes 1179656 | tf_op jit(solution)/shard_map/ppermute | solution.py:1026
  8.5 17.7 %collective-permute-start.1 = (bf16[256,768]{1,0:T(8,128)(2,1)}, bf16[256,768]{1,0:T(8,128)(2,1)S(1)}, u32[]{:S(2)}, u32[]{:S(2)}) collective-permute-start(bf16[256,768]{1,0:T(8,128)(2,1)} %get-tuple-element.78.refs_10_.refs_8_.refs_7_.refs_11_), channel_id=1, source_target_pairs={{0,16},{4,20},{8,24},{12,28},{16,0},{20,4},{24,8},{28,12},{1,17},{... | collective-permute-start | bytes 1179656 | tf_op jit(solution)/shard_map/ppermute | solution.py:1026
  9.0 17.5 %collective-permute-start = (bf16[256,768]{1,0:T(8,128)(2,1)}, bf16[256,768]{1,0:T(8,128)(2,1)S(1)}, u32[]{:S(2)}, u32[]{:S(2)}) collective-permute-start(bf16[256,768]{1,0:T(8,128)(2,1)} %get-tuple-element.78.refs_10_.refs_8_.refs_7_.refs_11_), channel_id=1, source_target_pairs={{0,8},{4,12},{8,0},{12,4},{16,24},{20,28},{24,16},{28,20},{1,9},{5... | collective-permute-start | bytes 1179656 | tf_op jit(solution)/shard_map/ppermute | solution.py:1026
  9.1 7.0 %collective-permute-start.5 = (bf16[112,576]{1,0:T(8,128)(2,1)}, bf16[112,576]{1,0:T(8,128)(2,1)S(1)}, u32[]{:S(2)}, u32[]{:S(2)}) collective-permute-start(bf16[112,576]{1,0:T(8,128)(2,1)} %get-tuple-element.80.refs_8_), channel_id=1, source_target_pairs={{0,1},{1,0},{2,3},{3,2},{4,5},{5,4},{6,7},{7,6},{8,9},{9,8},{10,11... | collective-permute-start | bytes 387080 | tf_op jit(solution)/shard_map/ppermute | solution.py:1029
  11.1 10.9 %collective-permute-start.4 = (bf16[112,576]{1,0:T(8,128)(2,1)}, bf16[112,576]{1,0:T(8,128)(2,1)S(1)}, u32[]{:S(2)}, u32[]{:S(2)}) collective-permute-start(bf16[112,576]{1,0:T(8,128)(2,1)} %get-tuple-element.80.refs_8_), channel_id=1, source_target_pairs={{0,2},{1,3},{2,0},{3,1},{4,6},{5,7},{6,4},{7,5},{8,10},{9,11},{10,... | collective-permute-start | bytes 387080 | tf_op jit(solution)/shard_map/ppermute | solution.py:1029
  16.1 7.5 %collective-permute-start.3 = (bf16[112,576]{1,0:T(8,128)(2,1)}, bf16[112,576]{1,0:T(8,128)(2,1)S(1)}, u32[]{:S(2)}, u32[]{:S(2)}) collective-permute-start(bf16[112,576]{1,0:T(8,128)(2,1)} %get-tuple-element.80.refs_8_), channel_id=1, source_target_pairs={{0,3},{1,2},{2,1},{3,0},{4,7},{5,6},{6,5},{7,4},{8,11},{9,10},{10,... | collective-permute-start | bytes 387080 | tf_op jit(solution)/shard_map/ppermute | solution.py:1029
  26.5 0.9 copy-start.5
  27.4 0.7 copy-start.6
  28.0 0.9 copy-start.11
  28.8 6.7 %collective-permute-start.10 = (bf16[384,576]{1,0:T(8,128)(2,1)S(1)}, bf16[384,576]{1,0:T(8,128)(2,1)S(1)}, u32[]{:S(2)}, u32[]{:S(2)}) collective-permute-start(bf16[384,576]{1,0:T(8,128)(2,1)S(1)} %get-tuple-element.84.refs_6_), channel_id=1, source_target_pairs={{0,4},{4,0},{8,12},{12,8},{16,20},{20,16},{24,28},{28,24},{1,5},{5... | collective-permute-start | bytes 1327112 | tf_op jit(solution)/shard_map/ppermute | solution.py:1026
  28.9 8.7 %collective-permute-start.11 = (bf16[96,768]{1,0:T(8,128)(2,1)S(1)}, bf16[96,768]{1,0:T(8,128)(2,1)S(1)}, u32[]{:S(2)}, u32[]{:S(2)}) collective-permute-start(bf16[96,768]{1,0:T(8,128)(2,1)S(1)} %copy-done.11), channel_id=1, source_target_pairs={{0,0},{1,1},{2,2},{3,3},{4,4},{5,5},{6,6},{7,7},{8,9},{9,8},{10,11... | collective-permute-start | bytes 442376 | tf_op jit(solution)/shard_map/ppermute | solution.py:1041
  29.6 13.6 %collective-permute-start.8 = (bf16[256,768]{1,0:T(8,128)(2,1)}, bf16[256,768]{1,0:T(8,128)(2,1)S(1)}, u32[]{:S(2)}, u32[]{:S(2)}) collective-permute-start(bf16[256,768]{1,0:T(8,128)(2,1)} %get-tuple-element.81.refs_16_), channel_id=1, source_target_pairs={{3,2},{2,1},{1,0},{7,6},{6,5},{5,4},{11,10},{10,9},{9,8},{15,14},{... | collective-permute-start | bytes 1179656 | tf_op jit(solution)/shard_map/ppermute | solution.py:1038
  30.9 13.6 %collective-permute-start.6 = (bf16[256,768]{1,0:T(8,128)(2,1)}, bf16[256,768]{1,0:T(8,128)(2,1)S(1)}, u32[]{:S(2)}, u32[]{:S(2)}) collective-permute-start(bf16[256,768]{1,0:T(8,128)(2,1)} %get-tuple-element.81.refs_16_), channel_id=1, source_target_pairs={{0,1},{1,2},{2,3},{4,5},{5,6},{6,7},{8,9},{9,10},{10,11},{12,13},{... | collective-permute-start | bytes 1179656 | tf_op jit(solution)/shard_map/ppermute | solution.py:1038
  37.5 7.6 %collective-permute-start.14 = (bf16[1024,192]{1,0:T(8,128)(2,1)S(1)}, bf16[1024,192]{1,0:T(8,128)(2,1)S(1)}, u32[]{:S(2)}, u32[]{:S(2)}) collective-permute-start(bf16[1024,192]{1,0:T(8,128)(2,1)S(1)} %get-tuple-element.90.refs_10_), channel_id=1, source_target_pairs={{0,4},{4,0},{8,12},{12,8},{16,20},{20,16},{24,28},{28,24},{1,5},{5... | collective-permute-start | bytes 1179656 | tf_op jit(solution)/shard_map/ppermute | solution.py:1026
  37.6 0.7 collective-permute-start.12
  38.3 6.8 %collective-permute-start.13 = (bf16[96,768]{1,0:T(8,128)(2,1)S(1)}, bf16[96,768]{1,0:T(8,128)(2,1)S(1)}, u32[]{:S(2)}, u32[]{:S(2)}) collective-permute-start(bf16[96,768]{1,0:T(8,128)(2,1)S(1)} %collective-permute-done.12.refs_4_), channel_id=1, source_target_pairs={{0,4},{4,0},{8,12},{12,8},{16,20},{20,16},{24,28},{28,24},{1,5},{5... | collective-permute-start | bytes 442376 | tf_op jit(solution)/shard_map/ppermute | solution.py:1026
  43.2 18.0 %collective-permute-start.9 = (bf16[256,768]{1,0:T(8,128)(2,1)S(1)}, bf16[256,768]{1,0:T(8,128)(2,1)S(1)}, u32[]{:S(2)}, u32[]{:S(2)}) collective-permute-start(bf16[256,768]{1,0:T(8,128)(2,1)S(1)} %collective-permute-done.8.refs_2_.refs_12_), channel_id=1, source_target_pairs={{2,1},{1,0},{6,5},{5,4},{10,9},{9,8},{14,13},{13,12},{18,17},{17,1... | collective-permute-start | bytes 1179656 | tf_op jit(solution)/shard_map/ppermute | solution.py:1038
  44.5 16.7 %collective-permute-start.7 = (bf16[256,768]{1,0:T(8,128)(2,1)S(1)}, bf16[256,768]{1,0:T(8,128)(2,1)S(1)}, u32[]{:S(2)}, u32[]{:S(2)}) collective-permute-start(bf16[256,768]{1,0:T(8,128)(2,1)S(1)} %collective-permute-done.6.refs_1_.refs_15_), channel_id=1, source_target_pairs={{1,2},{2,3},{5,6},{6,7},{9,10},{10,11},{13,14},{14,15},{17,18},{18... | collective-permute-start | bytes 1179656 | tf_op jit(solution)/shard_map/ppermute | solution.py:1038
  45.2 17.4 %copy-start.10 = (bf16[768]{0:T(1024)(128)(2,1)S(1)}, bf16[768]{0:T(1024)(128)(2,1)}, u32[]{:S(2)}) copy-start(bf16[768]{0:T(1024)(128)(2,1)} %param.27) | copy-start | bytes 4612
  45.2 28.6 %copy-start.1 = (bf16[1,128,768]{2,1,0:T(8,128)(2,1)S(1)}, bf16[1,128,768]{2,1,0:T(8,128)(2,1)}, u32[]{:S(2)}) copy-start(bf16[1,128,768]{2,1,0:T(8,128)(2,1)} %param.17) | copy-start | bytes 589828
  53.2 19.8 %collective-permute-start.15 = (bf16[512,384]{1,0:T(8,128)(2,1)S(1)}, bf16[512,384]{1,0:T(8,128)(2,1)S(1)}, u32[]{:S(2)}, u32[]{:S(2)}) collective-permute-start(bf16[512,384]{1,0:T(8,128)(2,1)S(1)} %get-tuple-element.92), channel_id=1, source_target_pairs={{0,4},{4,0},{8,12},{12,8},{16,20},{20,16},{24,28},{28,24},{1,5},{5... | collective-permute-start | bytes 1179656 | tf_op jit(solution)/shard_map/ppermute | solution.py:1026
  61.2 29.6 %collective-permute-start.20 = (bf16[256,768]{1,0:T(8,128)(2,1)S(1)}, bf16[256,768]{1,0:T(8,128)(2,1)S(1)}, u32[]{:S(2)}, u32[]{:S(2)}) collective-permute-start(bf16[256,768]{1,0:T(8,128)(2,1)S(1)} %add.3), channel_id=1, source_target_pairs={{2,3},{1,0},{6,7},{5,4},{10,11},{9,8},{14,15},{13,12},{18,19},{17,... | collective-permute-start | bytes 1179656 | tf_op jit(solution)/shard_map/ppermute | solution.py:1082
  62.6 13.9 %collective-permute-start.16 = (bf16[128,192]{1,0:T(8,128)(2,1)S(1)}, bf16[128,192]{1,0:T(8,128)(2,1)S(1)}, u32[]{:S(2)}, u32[]{:S(2)}) collective-permute-start(bf16[128,192]{1,0:T(8,128)(2,1)S(1)} %get-tuple-element.96), channel_id=1, source_target_pairs={{0,24},{1,16},{2,8},{3,0},{4,28},{5,20},{6,12},{7,4},{8,25},{9,17}... | collective-permute-start | bytes 147464 | tf_op jit(solution)/shard_map/ppermute | solution.py:1041
  65.5 11.1 %collective-permute-start.17 = (bf16[128,192]{1,0:T(8,128)(2,1)S(1)}, bf16[128,192]{1,0:T(8,128)(2,1)S(1)}, u32[]{:S(2)}, u32[]{:S(2)}) collective-permute-start(bf16[128,192]{1,0:T(8,128)(2,1)S(1)} %get-tuple-element.97), channel_id=1, source_target_pairs={{0,16},{1,24},{2,0},{3,8},{4,20},{5,28},{6,4},{7,12},{8,17},{9,25}... | collective-permute-start | bytes 147464 | tf_op jit(solution)/shard_map/ppermute | solution.py:1041
  71.2 19.5 %collective-permute-start.18 = (bf16[128,192]{1,0:T(8,128)(2,1)S(1)}, bf16[128,192]{1,0:T(8,128)(2,1)S(1)}, u32[]{:S(2)}, u32[]{:S(2)}) collective-permute-start(bf16[128,192]{1,0:T(8,128)(2,1)S(1)} %get-tuple-element.98), channel_id=1, source_target_pairs={{0,8},{1,0},{2,24},{3,16},{4,12},{5,4},{6,28},{7,20},{8,9},{9,1},{... | collective-permute-start | bytes 147464 | tf_op jit(solution)/shard_map/ppermute | solution.py:1041
  73.0 17.8 %collective-permute-start.19 = (bf16[128,192]{1,0:T(8,128)(2,1)S(1)}, bf16[128,192]{1,0:T(8,128)(2,1)S(1)}, u32[]{:S(2)}, u32[]{:S(2)}) collective-permute-start(bf16[128,192]{1,0:T(8,128)(2,1)S(1)} %get-tuple-element.99), channel_id=1, source_target_pairs={{0,0},{1,8},{2,16},{3,24},{4,4},{5,12},{6,20},{7,28},{8,1},{9,9},{... | collective-permute-start | bytes 147464 | tf_op jit(solution)/shard_map/ppermute | solution.py:1041
  73.8 17.0 %copy-start.4 = (bf16[192,768]{1,0:T(8,128)(2,1)S(1)}, bf16[192,768]{1,0:T(8,128)(2,1)}, u32[]{:S(2)}) copy-start(bf16[192,768]{1,0:T(8,128)(2,1)} %refs_6_.3) | copy-start | bytes 884740
  73.8 17.0 %copy-start.8 = (bf16[768,768]{1,0:T(8,128)(2,1)S(1)}, bf16[768,768]{1,0:T(8,128)(2,1)}, u32[]{:S(2)}) copy-start(bf16[768,768]{1,0:T(8,128)(2,1)} %refs_9_.3) | copy-start | bytes 3538948
  73.9 17.0 %copy-start.9 = (bf16[768,768]{1,0:T(8,128)(2,1)S(1)}, bf16[768,768]{1,0:T(8,128)(2,1)}, u32[]{:S(2)}) copy-start(bf16[768,768]{1,0:T(8,128)(2,1)} %refs_10_.3) | copy-start | bytes 3538948
  97.6 4.1 %collective-permute-start.21 = (bf16[912,768]{1,0:T(8,128)(2,1)S(1)}, bf16[912,768]{1,0:T(8,128)(2,1)S(1)}, u32[]{:S(2)}, u32[]{:S(2)}) collective-permute-start(bf16[912,768]{1,0:T(8,128)(2,1)S(1)} %get-tuple-element.109), channel_id=1, source_target_pairs={{0,4},{4,0},{8,12},{12,8},{16,20},{20,16},{24,28},{28,24},{1,5},{5... | collective-permute-start | bytes 4202504 | tf_op jit(solution)/shard_map/ppermute | solution.py:1026
  97.7 4.0 %collective-permute-start.22 = (bf16[4,112,576]{2,1,0:T(8,128)(2,1)S(1)}, bf16[4,112,576]{2,1,0:T(8,128)(2,1)S(1)}, u32[]{:S(2)}, u32[]{:S(2)}) collective-permute-start(bf16[4,112,576]{2,1,0:T(8,128)(2,1)S(1)} %get-tuple-element.110), channel_id=1, source_target_pairs={{0,4},{4,0},{8,12},{12,8},{16,20},{20,16},{24,28},{28,24},{1,5},{5... | collective-permute-start | bytes 1548296 | tf_op jit(solution)/shard_map/ppermute | solution.py:1026
  102.4 9.9 %collective-permute-start.23 = (bf16[112,576]{1,0:T(8,128)(2,1)S(1)}, bf16[112,576]{1,0:T(8,128)(2,1)S(1)}, u32[]{:S(2)}, u32[]{:S(2)}) collective-permute-start(bf16[112,576]{1,0:T(8,128)(2,1)S(1)} %get-tuple-element.111), channel_id=1, source_target_pairs={{0,3},{1,2},{2,1},{3,0},{4,7},{5,6},{6,5},{7,4},{8,11},{9,10},{10,... | collective-permute-start | bytes 387080 | tf_op jit(solution)/shard_map/ppermute | solution.py:1029
  108.6 16.2 %collective-permute-start.29 = (bf16[352,768]{1,0:T(8,128)(2,1)S(1)}, bf16[352,768]{1,0:T(8,128)(2,1)S(1)}, u32[]{:S(2)}, u32[]{:S(2)}) collective-permute-start(bf16[352,768]{1,0:T(8,128)(2,1)S(1)} %get-tuple-element.123), channel_id=1, source_target_pairs={{0,24},{4,28},{8,16},{12,20},{16,8},{20,12},{24,0},{28,4},{1,25},{... | collective-permute-start | bytes 1622024 | tf_op jit(solution)/shard_map/ppermute | solution.py:1026
  110.1 25.1 %collective-permute-start.30 = (bf16[352,768]{1,0:T(8,128)(2,1)S(1)}, bf16[352,768]{1,0:T(8,128)(2,1)S(1)}, u32[]{:S(2)}, u32[]{:S(2)}) collective-permute-start(bf16[352,768]{1,0:T(8,128)(2,1)S(1)} %get-tuple-element.124), channel_id=1, source_target_pairs={{0,16},{4,20},{8,24},{12,28},{16,0},{20,4},{24,8},{28,12},{1,17},{... | collective-permute-start | bytes 1622024 | tf_op jit(solution)/shard_map/ppermute | solution.py:1026
  110.9 25.0 %collective-permute-start.31 = (bf16[352,768]{1,0:T(8,128)(2,1)S(1)}, bf16[352,768]{1,0:T(8,128)(2,1)S(1)}, u32[]{:S(2)}, u32[]{:S(2)}) collective-permute-start(bf16[352,768]{1,0:T(8,128)(2,1)S(1)} %get-tuple-element.125), channel_id=1, source_target_pairs={{0,8},{4,12},{8,0},{12,4},{16,24},{20,28},{24,16},{28,20},{1,9},{5... | collective-permute-start | bytes 1622024 | tf_op jit(solution)/shard_map/ppermute | solution.py:1026
  112.2 6.7 %collective-permute-start.24 = (bf16[112,576]{1,0:T(8,128)(2,1)S(1)}, bf16[112,576]{1,0:T(8,128)(2,1)S(1)}, u32[]{:S(2)}, u32[]{:S(2)}) collective-permute-start(bf16[112,576]{1,0:T(8,128)(2,1)S(1)} %get-tuple-element.112), channel_id=1, source_target_pairs={{0,2},{1,3},{2,0},{3,1},{4,6},{5,7},{6,4},{7,5},{8,10},{9,11},{10,... | collective-permute-start | bytes 387080 | tf_op jit(solution)/shard_map/ppermute | solution.py:1029
  112.3 8.1 %collective-permute-start.25 = (bf16[112,576]{1,0:T(8,128)(2,1)S(1)}, bf16[112,576]{1,0:T(8,128)(2,1)S(1)}, u32[]{:S(2)}, u32[]{:S(2)}) collective-permute-start(bf16[112,576]{1,0:T(8,128)(2,1)S(1)} %get-tuple-element.113), channel_id=1, source_target_pairs={{0,1},{1,0},{2,3},{3,2},{4,5},{5,4},{6,7},{7,6},{8,9},{9,8},{10,11... | collective-permute-start | bytes 387080 | tf_op jit(solution)/shard_map/ppermute | solution.py:1029
  121.0 19.3 %collective-permute-start.26 = (bf16[256,768]{1,0:T(8,128)(2,1)S(1)}, bf16[256,768]{1,0:T(8,128)(2,1)S(1)}, u32[]{:S(2)}, u32[]{:S(2)}) collective-permute-start(bf16[256,768]{1,0:T(8,128)(2,1)S(1)} %get-tuple-element.115), channel_id=1, source_target_pairs={{0,3},{1,0},{2,1},{3,2},{4,7},{5,4},{6,5},{7,6},{8,11},{9,8},{10,9... | collective-permute-start | bytes 1179656 | tf_op jit(solution)/shard_map/ppermute | solution.py:1032
  136.7 28.5 %collective-permute-start.34 = (bf16[320,768]{1,0:T(8,128)(2,1)S(1)}, bf16[320,768]{1,0:T(8,128)(2,1)S(1)}, u32[]{:S(2)}, u32[]{:S(2)}) collective-permute-start(bf16[320,768]{1,0:T(8,128)(2,1)S(1)} %plane_share.1.refs_7_), channel_id=1, source_target_pairs={{0,8},{4,12},{8,0},{12,4},{16,24},{20,28},{24,16},{28,20},{1,9},{5... | collective-permute-start | bytes 1474568 | tf_op jit(solution)/shard_map/ppermute | solution.py:1026
  137.0 28.2 %collective-permute-start.33 = (bf16[320,768]{1,0:T(8,128)(2,1)S(1)}, bf16[320,768]{1,0:T(8,128)(2,1)S(1)}, u32[]{:S(2)}, u32[]{:S(2)}) collective-permute-start(bf16[320,768]{1,0:T(8,128)(2,1)S(1)} %plane_share.1.refs_7_), channel_id=1, source_target_pairs={{0,16},{4,20},{8,24},{12,28},{16,0},{20,4},{24,8},{28,12},{1,17},{... | collective-permute-start | bytes 1474568 | tf_op jit(solution)/shard_map/ppermute | solution.py:1026
  138.1 27.2 %collective-permute-start.32 = (bf16[320,768]{1,0:T(8,128)(2,1)S(1)}, bf16[320,768]{1,0:T(8,128)(2,1)S(1)}, u32[]{:S(2)}, u32[]{:S(2)}) collective-permute-start(bf16[320,768]{1,0:T(8,128)(2,1)S(1)} %plane_share.1.refs_7_), channel_id=1, source_target_pairs={{0,24},{4,28},{8,16},{12,20},{16,8},{20,12},{24,0},{28,4},{1,25},{... | collective-permute-start | bytes 1474568 | tf_op jit(solution)/shard_map/ppermute | solution.py:1026
  140.3 24.9 %collective-permute-start.27 = (bf16[256,768]{1,0:T(8,128)(2,1)S(1)}, bf16[256,768]{1,0:T(8,128)(2,1)S(1)}, u32[]{:S(2)}, u32[]{:S(2)}) collective-permute-start(bf16[256,768]{1,0:T(8,128)(2,1)S(1)} %get-tuple-element.116), channel_id=1, source_target_pairs={{0,2},{1,3},{2,0},{3,1},{4,6},{5,7},{6,4},{7,5},{8,10},{9,11},{10,... | collective-permute-start | bytes 1179656 | tf_op jit(solution)/shard_map/ppermute | solution.py:1032
  140.3 24.9 %collective-permute-start.28 = (bf16[256,768]{1,0:T(8,128)(2,1)S(1)}, bf16[256,768]{1,0:T(8,128)(2,1)S(1)}, u32[]{:S(2)}, u32[]{:S(2)}) collective-permute-start(bf16[256,768]{1,0:T(8,128)(2,1)S(1)} %get-tuple-element.117), channel_id=1, source_target_pairs={{0,1},{1,2},{2,3},{3,0},{4,5},{5,6},{6,7},{7,4},{8,9},{9,10},{10,1... | collective-permute-start | bytes 1179656 | tf_op jit(solution)/shard_map/ppermute | solution.py:1032
  165.9 4.0 %collective-permute-start.35 = (bf16[1280,768]{1,0:T(8,128)(2,1)S(1)}, bf16[1280,768]{1,0:T(8,128)(2,1)S(1)}, u32[]{:S(2)}, u32[]{:S(2)}) collective-permute-start(bf16[1280,768]{1,0:T(8,128)(2,1)S(1)} %stack.13.refs_1_.refs_2_), channel_id=1, source_target_pairs={{0,4},{4,0},{8,12},{12,8},{16,20},{20,16},{24,28},{28,24},{1,5},{5... | collective-permute-start | bytes 5898248 | tf_op jit(solution)/shard_map/ppermute | solution.py:1026
  166.0 4.0 %copy-start.7 = (s32[2]{0:T(128)S(1)}, s32[2]{0:T(128)}, u32[]{:S(2)}) copy-start(s32[2]{0:T(128)} %pad_add_fusion.refs_0_) | copy-start | bytes 28
